TPU v7x, 256 devices: a whole 4x4x8 slice. The times are simulated.
256 devices in a mesh: pb: 32 (over x, z_hi, core), ka: 8 (over z_lo, y).
Axes of the slice: x: 4, y: 4, z: 8 (z_hi: 4, z_lo: 2; z = z_hi * 2 + z_lo), core: 2. Of those that a mesh axis runs over, the one named last changes fastest.
Arguments:
- frame_two: bfloat16 [96, 1024, 4096], P(None, 'pb', 'ka'), may hold values from -24 to 24
- frame_band: bfloat16 [96, 9, 4096], P(None, None, 'pb'), may hold values from -24 to 24
- conv_weight: bfloat16 [9, 128, 96], replicated, may hold values from -0.21875 to 0.21875
Outputs:
- flow: float32 [2, 4, 2048], P(None, None, 'pb')
All inputs are finite; a program needn't handle non-finite values.
Results may differ from a plain program's by a relative error of at most 0.0035.
The roundings to bfloat16 on the way count: a program that leaves them out, or rounds other values in their place, can miss the bound.
Values may be sent and summed in bfloat16 or wider, within the bound.
No kernel may reach another device: no remote copies, remote signals or barrier semaphores. Data moves between devices by JAX's collectives and lax.ppermute only.
A program may use at most 192 MiB of HBM per device.

v0:
```python
import math

import jax
import jax.numpy as jnp
from jax import lax
from jax.sharding import PartitionSpec as P


def passed_along(x, axis, by):
    count = lax.axis_size(axis)
    pairs = [(i, i + by) for i in range(count) if 0 <= i + by < count]
    return lax.ppermute(x, axis, pairs)


def combined_all(part, axis, combine):
    gathered = jax.tree.map(lambda a: lax.all_gather(a, axis), part)

    def take(source):
        return jax.tree.map(lambda a: lax.dynamic_index_in_dim(a, source, 0, False), gathered)

    return lax.fori_loop(
        1, lax.axis_size(axis), lambda source, state: combine(state, take(source)), take(0)
    )


def conv_planes(padded, weight_matrix, out_rows, out_cols):
    channels_in = padded.shape[0]
    extended = jnp.pad(
        padded,
        ((0, 0), (0, 2 * out_rows + 2 - padded.shape[1]), (0, 2 * out_cols + 2 - padded.shape[2])),
    )
    planes = extended.reshape(channels_in, out_rows + 1, 2, out_cols + 1, 2).transpose(
        2, 4, 0, 1, 3
    )
    windows = []
    for tap_index in range(9):
        row_off = tap_index // 3
        col_off = tap_index % 3
        plane = planes[row_off % 2, col_off % 2]
        windows.append(
            plane[:, row_off // 2 : row_off // 2 + out_rows, col_off // 2 : col_off // 2 + out_cols]
        )
    stacked = jnp.concatenate(windows, axis=0).reshape(9 * channels_in, out_rows * out_cols)
    total = jnp.dot(weight_matrix, stacked, preferred_element_type=jnp.float32)
    return total.astype(jnp.bfloat16)


def combine(first, second):
    highest = jnp.maximum(first[0], second[0])
    left_w = jnp.exp(first[0] - highest)
    right_w = jnp.exp(second[0] - highest)
    return (
        highest,
        first[1] * left_w + second[1] * right_w,
        first[2] * left_w + second[2] * right_w,
        first[3] * left_w + second[3] * right_w,
    )


def block_states(queries, key_block, key_x, key_y, factor):
    scores = (
        lax.dot_general(
            queries, key_block, (((0,), (0,)), ((), ())), preferred_element_type=jnp.float32
        )
        * factor
    )
    highest = jnp.max(scores, axis=1)
    weights = jnp.exp(scores - highest[:, None])
    return (
        highest,
        jnp.sum(weights, axis=1),
        jnp.sum(weights * key_x[None, :], axis=1),
        jnp.sum(weights * key_y[None, :], axis=1),
    )


def empty_states(length):
    return (
        jnp.full((length,), -jnp.inf, jnp.float32),
        jnp.zeros((length,), jnp.float32),
        jnp.zeros((length,), jnp.float32),
        jnp.zeros((length,), jnp.float32),
    )


def bounded_states(queries, key_feats, key_x, key_y, factor):
    n_query = queries.shape[1]
    n_key = key_feats.shape[1]
    qblk = math.gcd(n_query, 512)
    kblk = math.gcd(n_key, 4096)

    def per_query(query_index):

        def step(running, index):
            offset = index * kblk
            feats = lax.dynamic_slice_in_dim(key_feats, offset, kblk, 1)
            block_x = lax.dynamic_slice_in_dim(key_x, offset, kblk, 0)
            block_y = lax.dynamic_slice_in_dim(key_y, offset, kblk, 0)
            return (combine(running, block_states(queries, feats, block_x, block_y, factor)), None)

        final, unused = lax.scan(
            step, empty_states(qblk), jnp.arange(n_key // kblk, dtype=jnp.int32)
        )
        return final

    results = lax.map(per_query, jnp.arange(n_query // qblk, dtype=jnp.int32))
    return tuple((part.reshape(n_query) for part in results))


def on_device(frame_two, frame_band, conv_weight):
    tile_rows = frame_two.shape[1] // 2
    tile_cols = frame_two.shape[2] // 2
    band_rows = (frame_band.shape[1] - 1) // 2
    band_cols = frame_band.shape[2] // 2
    channels = conv_weight.shape[1]
    channels_in = conv_weight.shape[2]
    weight_matrix = conv_weight.transpose(1, 0, 2).reshape(channels, 9 * channels_in)
    row_count = tile_rows * lax.axis_size("pb")
    col_count = tile_cols * lax.axis_size("ka")
    pb_index = lax.axis_index("pb")
    ka_index = lax.axis_index("ka")
    row_above, band_left = passed_along((frame_two[:, -1:, :], frame_band[:, :, -1:]), "pb", 1)
    taller = jnp.concatenate([row_above, frame_two], axis=1)
    col_left = passed_along(taller[:, :, -1:], "ka", 1)
    padded_two = jnp.concatenate([col_left, taller], axis=2)
    key_feats = conv_planes(padded_two, weight_matrix, tile_rows, tile_cols).reshape(
        channels, tile_rows, tile_cols
    )
    padded_band = jnp.concatenate([band_left, frame_band], axis=2)
    query_feats = conv_planes(padded_band, weight_matrix, band_rows, band_cols)
    n_query = band_rows * band_cols
    factor = 1.0 / math.sqrt(channels)
    col_coords = (
        2.0 * (ka_index * tile_cols + jnp.arange(tile_cols, dtype=jnp.int32)).astype(jnp.float32)
        + 1.0
    ) / col_count - 1.0
    shard_rows = lax.all_gather(key_feats, "pb", axis=1, tiled=True)
    count = shard_rows.shape[1]
    row_coords = (
        2.0 * jnp.arange(count, dtype=jnp.int32).astype(jnp.float32) + 1.0
    ) / row_count - 1.0
    flat_keys = shard_rows.reshape(channels, count * tile_cols)
    key_y = jnp.repeat(row_coords, tile_cols)
    key_x = jnp.tile(col_coords, count)
    partial_states = combine(
        empty_states(n_query), bounded_states(query_feats, flat_keys, key_x, key_y, factor)
    )
    states = combined_all(partial_states, "ka", combine)
    mean_x = (states[2] / states[1]).reshape(band_rows, band_cols)
    mean_y = (states[3] / states[1]).reshape(band_rows, band_cols)
    query_x = (
        2.0 * (pb_index * band_cols + jnp.arange(band_cols, dtype=jnp.int32)).astype(jnp.float32)
        + 1.0
    ) / col_count - 1.0
    band_top = (row_count - band_rows) // 2
    query_y = (
        2.0 * (band_top + jnp.arange(band_rows, dtype=jnp.int32)).astype(jnp.float32) + 1.0
    ) / row_count - 1.0
    return jnp.stack([mean_x - query_x[None, :], mean_y - query_y[:, None]])


def solution(mesh):
    in_specs = (P(None, "pb", "ka"), P(None, None, "pb"), P())
    out_specs = P(None, None, "pb")
    return jax.shard_map(
        on_device, mesh=mesh, in_specs=in_specs, out_specs=out_specs, check_vma=False
    )
```

profile of v0, /device:TPU:44, one launch (start us, length us, event | category | flops | bytes accessed | tf_op | source)
XLA Modules:
  0.0 587.8 jit_solution(11653148774546687125)
XLA Ops:
  9.9 8.6 %copy.43 = bf16[96,32,512]{0,1,2:T(8,128)(2,1)} copy(bf16[96,32,512]{2,1,0:T(8,128)(2,1)} %param.7) | data formatting | bytes 6291456 | tf_op args[0]
  19.5 3.6 collective-permute-start.1
  25.2 6.4 %fusion.14 = bf16[96,34,514]{0,1,2:T(8,128)(2,1)} fusion(bf16[96,33,1]{0,1,2:T(8,128)(2,1)S(1)} %collective-permute-done.1, bf16[96,32,512]{0,1,2:T(8,128)(2,1)S(1)} %copy-done.2, bf16[96,1,512]{0,1,2:T(2,128)(2,1)S(1)} %copy.42), kind=kLoop, calls=%fused_computation.35 | loop fusion | flops 25165440 | bytes 6605760 | tf_op jit(solution)/shard_map/concatenate | solution.py:125
  31.6 10.3 %reshape.169 = bf16[96,17,2,257,2]{0,2,1,4,3:T(2,128)(2,1)} reshape(bf16[96,34,514]{0,1,2:T(8,128)(2,1)} %fusion.14) | data formatting | bytes 6710784 | tf_op jit(solution)/shard_map/reshape | solution.py:32
  41.9 7.8 %copy.81 = bf16[96,17,2,257,2]{0,4,3,2,1:T(2,128)(2,1)} copy(bf16[96,17,2,257,2]{0,2,1,4,3:T(2,128)(2,1)} %reshape.169) | data formatting | bytes 6710784 | tf_op jit(solution)/shard_map/reshape | solution.py:32
  49.7 9.5 %fusion.19 = (bf16[1,1,96,17,257]{2,1,4,0,3:T(2,128)(2,1)S(1)}, bf16[1,1,96,17,257]{2,1,4,0,3:T(2,128)(2,1)S(1)}, bf16[1,1,96,17,257]{2,1,4,0,3:T(2,128)(2,1)S(1)}, bf16[1,1,96,17,257]{2,1,4,0,3:T(2,128)(2,1)S(1)}) fusion(bf16[2,2,96,17,257]{2,1,4,0,3:T(2,128)(2,1)} %bitcast.86), kind=kLoop, calls=%fused_computation.70 | loop fusion | bytes 6710784 | tf_op jit(solution)/shard_map/slice | solution.py:39
  59.5 2.4 fusion.20
  65.0 12.8 %concatenate.17 = bf16[864,16,256]{0,2,1:T(8,128)(2,1)} concatenate(bf16[96,16,256]{0,2,1:T(8,128)(2,1)} %get-tuple-element.481, bf16[96,16,256]{0,2,1:T(8,128)(2,1)} %get-tuple-element.483, bf16[96,16,256]{0,2,1:T(8,128)(2,1)} %get-tuple-element.480, bf16[96,16,256]{0,2,1:T(8,128)(2,1)S(1)} %get-tuple-element.485, bf16[96,16,256]{0,2,1:T(8,128)(2,1)S(1)} %slice.146, ...), dimensions={0} | concatenate | bytes 14155776 | tf_op jit(solution)/shard_map/concatenate | solution.py:43
  77.8 5.2 convolution_convert_fusion
  84.5 4.1 collective-permute-start.2
  89.5 7.2 %collective-permute-done.2 = bf16[96,9,1]{2,0,1:T(8,128)(2,1)S(1)} collective-permute-done((bf16[96,9,1]{2,0,1:T(8,128)(2,1)S(1)}, bf16[96,9,1]{2,0,1:T(8,128)(2,1)S(1)}, u32[]{:S(2)}, u32[]{:S(2)}) %collective-permute-start.2) | collective-permute-done | bytes 1760 | tf_op jit(solution)/shard_map/ppermute | solution.py:12
  99.1 191.2 %all-gather.10.cloned.1.call-done = bf16[128,512,256]{2,0,1:T(8,128)(2,1)} async-done(((bf16[128,16,256]{2,0,1:T(8,128)(2,1)}), bf16[128,512,256]{2,0,1:T(8,128)(2,1)}) %all-gather.10.cloned.1.call-update) | async-done | bytes 33554448 | tf_op jit(solution)/shard_map/all_gather | solution.py:137
  290.3 43.8 %copy.46 = bf16[128,512,256]{0,2,1:T(8,128)(2,1)} copy(bf16[128,512,256]{2,0,1:T(8,128)(2,1)} %all-gather.10.cloned.1.call-done) | data formatting | bytes 67108864 | tf_op jit(solution)/shard_map/all_gather | solution.py:137
  334.1 177.8 %while.52 = (s32[]{:T(128)}, f32[256]{0:T(256)S(1)}, f32[256]{0:T(256)S(1)}, f32[256]{0:T(256)S(1)}, f32[256]{0:T(256)S(1)}, /*index=5*/s32[32]{0:T(128)S(1)}, b...) while((s32[]{:T(128)}, f32[256]{0:T(256)S(1)}, ...), condition=%wide.region_5.6_spmd.clone, body=%wide.region_0.5_spmd.clone.sunk | while | flops 276827904 | bytes 9623766 | solution.py:101
  337.3 2.3 multiply_reduce_fusion.3
  342.9 2.3 multiply_reduce_fusion.3
  348.4 2.3 multiply_reduce_fusion.3
  354.0 2.3 multiply_reduce_fusion.3
  359.6 2.3 multiply_reduce_fusion.3
  365.1 2.3 multiply_reduce_fusion.3
  370.7 2.3 multiply_reduce_fusion.3
  376.2 2.3 multiply_reduce_fusion.3
  381.8 2.3 multiply_reduce_fusion.3
  387.3 2.3 multiply_reduce_fusion.3
  392.9 2.3 multiply_reduce_fusion.3
  398.5 2.3 multiply_reduce_fusion.3
  404.0 2.3 multiply_reduce_fusion.3
  409.6 2.3 multiply_reduce_fusion.3
  415.1 2.3 multiply_reduce_fusion.3
  420.7 2.3 multiply_reduce_fusion.3
  426.2 2.3 multiply_reduce_fusion.3
  431.8 2.3 multiply_reduce_fusion.3
  437.4 2.3 multiply_reduce_fusion.3
  442.9 2.3 multiply_reduce_fusion.3
  448.5 2.3 multiply_reduce_fusion.3
  454.0 2.3 multiply_reduce_fusion.3
  459.6 2.3 multiply_reduce_fusion.3
  465.2 2.3 multiply_reduce_fusion.3
  470.7 2.3 multiply_reduce_fusion.3
  476.3 2.3 multiply_reduce_fusion.3
  481.8 2.3 multiply_reduce_fusion.3
  487.4 2.3 multiply_reduce_fusion.3
  498.5 2.3 multiply_reduce_fusion.3
  504.1 2.3 multiply_reduce_fusion.3
  512.0 16.1 %all-gather.5 = f32[8,1,256]{2,1,0:T(1,128)S(1)} all-gather(f32[1,1,256]{2,1,0:T(1,128)S(1)} %bitcast.109), channel_id=3, replica_groups=mesh['pb'=32,'ka'=8] {'ka'}, dimensions={0}, use_global_device_ids=true | all-gather | bytes 9216 | tf_op jit(solution)/shard_map/all_gather | solution.py:16
  528.0 19.2 %all-gather.6 = f32[8,1,256]{2,1,0:T(1,128)S(1)} all-gather(f32[1,1,256]{2,1,0:T(1,128)S(1)} %bitcast.108), channel_id=4, replica_groups=mesh['pb'=32,'ka'=8] {'ka'}, dimensions={0}, use_global_device_ids=true | all-gather | bytes 9216 | tf_op jit(solution)/shard_map/all_gather | solution.py:16
  547.3 15.1 %all-gather.7 = f32[8,1,256]{2,1,0:T(1,128)S(1)} all-gather(f32[1,1,256]{2,1,0:T(1,128)S(1)} %bitcast.107), channel_id=5, replica_groups=mesh['pb'=32,'ka'=8] {'ka'}, dimensions={0}, use_global_device_ids=true | all-gather | bytes 9216 | tf_op jit(solution)/shard_map/all_gather | solution.py:16
  562.3 17.1 %all-gather.4 = f32[8,1,256]{2,1,0:T(1,128)S(1)} all-gather(f32[1,1,256]{2,1,0:T(1,128)S(1)} %bitcast.95), channel_id=2, replica_groups=mesh['pb'=32,'ka'=8] {'ka'}, dimensions={0}, use_global_device_ids=true | all-gather | bytes 9216 | tf_op jit(solution)/shard_map/all_gather | solution.py:16
  (328 shorter events, 106.7 us)
Async XLA Ops:
  6.5 71.3 %copy-start = (bf16[9,128,96]{1,2,0:T(8,128)(2,1)S(1)}, bf16[9,128,96]{1,2,0:T(8,128)(2,1)}, u32[]{:S(2)}) copy-start(bf16[9,128,96]{1,2,0:T(8,128)(2,1)} %param.9) | copy-start | bytes 663556
  6.5 283.8 %all-gather.10.cloned.1.call-start = ((), (), s32[]{:S(2)}) async-start(), calls=%async_computation | async-start | bytes 34603008 | tf_op jit(solution)/shard_map/all_gather | solution.py:137
  7.9 10.5 %collective-permute-start = (bf16[96,1,512]{2,0,1:T(8,128)(2,1)S(1)}, bf16[96,1,512]{2,0,1:T(8,128)(2,1)S(1)}, u32[]{:S(2)}, u32[]{:S(2)}) collective-permute-start(bf16[96,1,512]{2,0,1:T(8,128)(2,1)S(1)} %copy.64), channel_id=1, source_target_pairs={{0,8},{8,16},{16,24},{24,32},{32,40},{40,48},{48,56},{56,64},{64,7... | collective-permute-start | bytes 294920 | tf_op jit(solution)/shard_map/ppermute | solution.py:12
  18.6 6.6 %copy-start.2 = (bf16[96,32,512]{0,1,2:T(8,128)(2,1)S(1)}, bf16[96,32,512]{0,1,2:T(8,128)(2,1)}, u32[]{:S(2)}) copy-start(bf16[96,32,512]{0,1,2:T(8,128)(2,1)} %copy.43) | copy-start | bytes 9437188
  19.5 5.7 collective-permute-start.1
  77.8 6.6 %copy-start.3 = (bf16[96,9,128]{2,0,1:T(8,128)(2,1)S(1)}, bf16[96,9,128]{2,0,1:T(8,128)(2,1)}, u32[]{:S(2)}) copy-start(bf16[96,9,128]{2,0,1:T(8,128)(2,1)} %param.8) | copy-start | bytes 663556
  84.5 12.2 %collective-permute-start.2 = (bf16[96,9,1]{2,0,1:T(8,128)(2,1)S(1)}, bf16[96,9,1]{2,0,1:T(8,128)(2,1)S(1)}, u32[]{:S(2)}, u32[]{:S(2)}) collective-permute-start(bf16[96,9,1]{2,0,1:T(8,128)(2,1)S(1)} %slice.116), channel_id=1, source_target_pairs={{0,8},{8,16},{16,24},{24,32},{32,40},{40,48},{48,56},{56,64},{64,7... | collective-permute-start | bytes 5192 | tf_op jit(solution)/shard_map/ppermute | solution.py:12
  511.9 69.1 %copy-start.1 = (bf16[9,128,96]{1,2,0:T(8,128)(2,1)S(1)}, bf16[9,128,96]{1,2,0:T(8,128)(2,1)}, u32[]{:S(2)}) copy-start(bf16[9,128,96]{1,2,0:T(8,128)(2,1)} %param.9) | copy-start | bytes 663556
Sparse Core Ops, SparseCore 0:
  84.5 205.7 all-gather.9
where the time goes:
time: 592 us; the launch traced here: 588 us
  waiting for transfers between devices  201 us (34%)
  local copies, waits for them, and re-layouts  123 us (21%)
  other arithmetic  82 us (14%)
  matrix products  71.6 us (12%)
  blocking collectives  67.5 us (11%)
  loops' own time  19.9 us (3%)
  between operations  13.7 us (2%)
  starting transfers between devices  9.66 us (2%)
    all_gather x1, waiting for transfers between devices, on_device(): shard_rows = lax.all_gather(key_feats, 'pb', axis=1, tiled=True)  191 us
    reduce_sum x32, other arithmetic, block_states(): jnp.sum(weights * key_y[None, :], axis=1)  72.3 us
    all_gather x4, blocking collectives, combined_all(): gathered = jax.tree.map(lambda a: lax.all_gather(a, axis), part)  67.5 us
    dot_general x32, matrix products, block_states(): lax.dot_general(queries, key_block, (((0,), (0,)), ((), ())), preferred_e...  66.1 us
    all_gather x1, local copies, waits for them, and re-layouts, on_device(): shard_rows = lax.all_gather(key_feats, 'pb', axis=1, tiled=True)  43.8 us
    another operation x1, loops' own time, per_query(): lax.scan(step, empty_states(qblk), jnp.arange(n_key // kblk, dtype=jnp.in...  19.6 us
    reshape x3, local copies, waits for them, and re-layouts, conv_planes(): extended.reshape(channels_in, out_rows + 1, 2, out_cols + 1, 2)  18.5 us
    dynamic_slice x32, local copies, waits for them, and re-layouts, per_query(): lax.scan(step, empty_states(qblk), jnp.arange(n_key // kblk, dtype=jnp.in...  17.8 us
  transfers between devices with their start and end apart: 4, of which 3 were waited for; matrix products, arithmetic and copies ran while one was open for 2% of the time, Pallas kernels for 0%

commit v1 on v0

v1 whole, which is shorter than its diff:
```python
import functools
import math

import jax
import jax.numpy as jnp
from jax import lax
from jax.experimental import pallas as pl
from jax.experimental.pallas import tpu as pltpu
from jax.sharding import PartitionSpec as P

BF16 = jnp.bfloat16
F32 = jnp.float32
GROUP = 8
TAIL = 32
VMEM = 56 * 1024 * 1024


def dot(a, b):
    return jnp.dot(a, b, preferred_element_type=F32)


def dot_nt(a, b):
    return lax.dot_general(a, b, (((1,), (1,)), ((), ())), preferred_element_type=F32)


def iota(shape, axis):
    return lax.broadcasted_iota(jnp.int32, shape, axis)


def tap_selector(cols):
    half = cols // 2
    row = iota((3 * half, cols), 0)
    tap = row // half
    source = 2 * (row - tap * half) - 1 + tap
    return (iota((3 * half, cols), 1) == source).astype(BF16)


def split3(x):
    high = x.astype(BF16)
    rest = x - high.astype(F32)
    mid = rest.astype(BF16)
    low = (rest - mid.astype(F32)).astype(BF16)
    return high, mid, low


def query_kernel(band_ref, w_ref, out_ref):
    rows_in, _, cols = band_ref.shape
    rows = (rows_in - 1) // 2
    half = cols // 2
    n_query = rows * half
    channels = w_ref.shape[2]
    selector = tap_selector(cols)
    picked = [dot_nt(selector, band_ref[r]).astype(BF16) for r in range(rows_in)]
    total = jnp.zeros((n_query, channels), F32)
    beyond = jnp.zeros((rows * 16, channels), F32)
    for a in range(3):
        for b in range(3):
            lhs = jnp.concatenate(
                [picked[2 * r + a][b * half : (b + 1) * half] for r in range(rows)], axis=0
            )
            total = total + dot(lhs, w_ref[3 * a + b])
        last = jnp.concatenate(
            [picked[2 * r + a][3 * half - 16 : 3 * half] for r in range(rows)], axis=0
        )
        beyond = beyond + dot(last, w_ref[3 * a])
    out_ref[0:n_query, :] = total.astype(BF16)
    edge = jnp.concatenate(
        [total[r * half : r * half + 1] for r in range(rows)]
        + [beyond[r * 16 + 15 : r * 16 + 16] for r in range(rows)],
        axis=0,
    )
    high, mid, low = split3(edge)
    tail = jnp.concatenate(
        [high.astype(F32), mid.astype(F32), low.astype(F32), jnp.zeros_like(edge)], axis=0
    )
    out_ref[n_query:, :] = tail.astype(BF16)


def key_kernel(x_ref, w_ref, key_ref, top_ref, left_ref, below_ref, right_ref, band_ref):
    channels_in, rows_in, cols = x_ref.shape
    half = cols // 2
    channels = w_ref.shape[2]
    depth = channels_in * GROUP
    outs = GROUP // 2
    n_group = rows_in // GROUP
    expand = (iota((depth, channels_in), 0) // GROUP == iota((depth, channels_in), 1)).astype(BF16)
    row = iota((depth, channels), 0) % GROUP
    for b in range(3):
        spread = [dot(expand, w_ref[3 * a + b]) for a in range(3)]
        for i in range(outs + 1):
            block = jnp.zeros((depth, channels), F32)
            for a in range(3):
                block = jnp.where(row == 2 * i - 1 + a, spread[a], block)
            band_ref[b, :, i * channels : (i + 1) * channels] = block.astype(BF16)
    selector = tap_selector(cols)
    carried = jnp.zeros((half, channels), F32)
    carried_right = jnp.zeros((1, channels), F32)
    for g in range(n_group):
        base = (g * GROUP) // 16 * 16
        pair = x_ref[:, base : base + 16, :].astype(F32)
        off = g * GROUP - base
        x = pair[:, off : off + GROUP, :].reshape(depth, cols).astype(BF16)
        picked = dot_nt(selector, x).astype(BF16)
        total = dot(picked[0:half], band_ref[0])
        total = total + dot(picked[half : 2 * half], band_ref[1])
        total = total + dot(picked[2 * half : 3 * half], band_ref[2])
        beyond = dot(picked[3 * half - 16 : 3 * half], band_ref[0])
        for i in range(outs):
            part = total[:, i * channels : (i + 1) * channels]
            part_right = beyond[15:16, i * channels : (i + 1) * channels]
            if i == 0:
                part = part + carried
                part_right = part_right + carried_right
            o = g * outs + i
            key_ref[o * half : (o + 1) * half, :] = part.astype(BF16)
            left_ref[o] = part[0:8]
            right_ref[o : o + 1, :] = part_right
            if o == 0:
                top_ref[...] = part
        carried = total[:, outs * channels :]
        carried_right = beyond[15:16, outs * channels :]
    below_ref[0:half, :] = carried
    below_ref[half:, :] = jnp.broadcast_to(carried_right, (8, channels))


def sum_tree(parts):
    while len(parts) > 1:
        rest = [parts[-1]] if len(parts) % 2 else []
        parts = [a + b for a, b in zip(parts[0::2], parts[1::2])] + rest
    return parts[0]


def bit_tree(parts):
    if len(parts) == 1:
        return parts[0], []
    middle = len(parts) // 2
    low, low_bits = bit_tree(parts[:middle])
    high, high_bits = bit_tree(parts[middle:])
    return low + high, [a + b for a, b in zip(low_bits, high_bits)] + [high]


def attention_kernel(
    tile_rows, row_count, col_count, scale,
    place_ref, query_ref, key_ref, top_ref, left_ref, above_ref, side_ref, corner_ref, out_ref,
    keys, ext, qt,
):
    step = pl.program_id(0)
    n_block = query_ref.shape[0]
    channels = key_ref.shape[1]
    tile_cols = key_ref.shape[0] // tile_rows
    n_query = query_ref.shape[1] - TAIL
    rows = 4
    half = n_query // rows
    width = n_block * n_query

    @pl.when(step == 0)
    def _():
        ext[...] = jnp.zeros_like(ext)
        keys[...] = key_ref[...]
        top = top_ref[...] + above_ref[0:tile_cols, :]
        first = jnp.broadcast_to(side_ref[0:1, :] + corner_ref[0:1, :], top.shape)
        top = jnp.where(iota(top.shape, 0) == 0, top + first, top)
        keys[0:tile_cols, :] = top.astype(BF16)
        for i in range(1, tile_rows):
            edge = left_ref[i][0:1, :] + side_ref[i : i + 1, :]
            old = keys[i * tile_cols : i * tile_cols + 16, :].astype(F32)
            new = jnp.where(iota(old.shape, 0) == 0, jnp.broadcast_to(edge, old.shape), old)
            keys[i * tile_cols : i * tile_cols + 16, :] = new.astype(BF16)

    for p in range(n_block):
        block = query_ref[p]
        tail = block[n_query:].astype(F32)
        edge = tail[0:8] + tail[8:16] + tail[16:24]
        fixed = edge + pltpu.roll(ext[...], 4, 0)
        ext[...] = edge
        pieces = []
        for r in range(rows):
            old = block[r * half : r * half + 16].astype(F32)
            new = jnp.where(
                iota(old.shape, 0) == 0, jnp.broadcast_to(fixed[r : r + 1], old.shape), old
            )
            pieces += [new.astype(BF16), block[r * half + 16 : (r + 1) * half]]
        qt[:, p * n_query : (p + 1) * n_query] = jnp.concatenate(pieces, axis=0).T

    def scores(start, count):
        return dot(keys[pl.ds(start, count), :], qt[...])

    def write(highest, states):
        total, down, bits = states
        along = sum(float(2**b) * x for b, x in enumerate(bits))
        sub = iota(total.shape, 0).astype(F32)
        first_row = place_ref[0].astype(F32)
        first_col = place_ref[1].astype(F32)
        x = ((2.0 * (first_col + sub) + 1.0) / col_count - 1.0) * total + (16.0 / col_count) * along
        y = ((2.0 * first_row + 1.0) / row_count - 1.0) * total + (2.0 / row_count) * down
        parts = [highest] + [jnp.sum(v, axis=0, keepdims=True) for v in (total, x, y)]
        for p in range(n_block):
            lanes = slice(p * n_query, (p + 1) * n_query)
            out_ref[p] = jnp.concatenate([v[:, lanes] for v in parts], axis=0)

    def add_row(i, start, shift, states):
        total, down, bits = states
        weights = jnp.exp2(scores(start, tile_cols) * scale - shift)
        row_total, row_bits = bit_tree([weights[8 * g : 8 * g + 8] for g in range(tile_cols // 8)])
        return (
            total + row_total,
            down + i * row_total,
            tuple(a + b for a, b in zip(bits, row_bits)),
        )

    zero = jnp.zeros((8, width), F32)
    empty = (zero, zero, (zero,) * int(math.log2(tile_cols // 8)))

    sample = jnp.concatenate(
        [keys[i * tile_cols : i * tile_cols + 16, :] for i in range(tile_rows)], axis=0
    )
    highest = jnp.max(dot(sample, qt[...]), axis=0, keepdims=True) * scale
    states = empty
    for i in range(tile_rows):
        states = add_row(float(i), i * tile_cols, highest, states)
    write(highest, states)
    largest = jnp.max(states[0])

    @pl.when(jnp.logical_not(largest < 1e30))
    def _():
        def raise_max(i, top):
            start = pl.multiple_of(i * tile_cols, tile_cols)
            return jnp.maximum(top, jnp.max(scores(start, tile_cols), axis=0, keepdims=True))

        top = lax.fori_loop(0, tile_rows, raise_max, jnp.full((1, width), -jnp.inf, F32)) * scale

        def again(i, states):
            start = pl.multiple_of(i * tile_cols, tile_cols)
            return add_row(i.astype(F32), start, top, states)

        write(top, lax.fori_loop(0, tile_rows, again, empty))


def whole(shape):
    return pl.BlockSpec(shape, lambda *_: (0,) * len(shape))


def merged(states):
    highest = jnp.max(states[:, 0], axis=0)
    factor = jnp.exp2(states[:, 0] - highest[None])
    sums = jnp.sum(states[:, 1:] * factor[:, None], axis=0)
    return jnp.concatenate([highest[None], sums], axis=0)


def on_device(frame_two, frame_band, conv_weight):
    channels_in, rows_in, cols_in = frame_two.shape
    channels = conv_weight.shape[1]
    tile_rows, tile_cols = rows_in // 2, cols_in // 2
    band_rows, band_cols = (frame_band.shape[1] - 1) // 2, frame_band.shape[2] // 2
    n_pb, n_ka = lax.axis_size("pb"), lax.axis_size("ka")
    row_count, col_count = tile_rows * n_pb, tile_cols * n_ka
    pb_index, ka_index = lax.axis_index("pb"), lax.axis_index("ka")
    n_query = band_rows * band_cols
    weights = conv_weight.transpose(0, 2, 1)
    params = pltpu.CompilerParams(vmem_limit_bytes=VMEM)

    queries = pl.pallas_call(
        query_kernel,
        out_shape=jax.ShapeDtypeStruct((n_query + TAIL, channels), BF16),
        compiler_params=params,
        name="query_feats",
    )(frame_band.transpose(1, 0, 2), weights)
    queries = lax.all_gather(queries, "pb")

    n_key = tile_rows * tile_cols
    keys, top, left, below, right = pl.pallas_call(
        key_kernel,
        out_shape=(
            jax.ShapeDtypeStruct((n_key, channels), BF16),
            jax.ShapeDtypeStruct((tile_cols, channels), F32),
            jax.ShapeDtypeStruct((tile_rows, 8, channels), F32),
            jax.ShapeDtypeStruct((tile_cols + 8, channels), F32),
            jax.ShapeDtypeStruct((tile_rows, channels), F32),
        ),
        scratch_shapes=[
            pltpu.VMEM((3, channels_in * GROUP, (GROUP // 2 + 1) * channels), BF16)
        ],
        compiler_params=params,
        name="key_feats",
    )(frame_two, weights)
    above = lax.ppermute(below, "pb", [(i, i + 1) for i in range(n_pb - 1)])
    side = lax.ppermute(right, "ka", [(i, i + 1) for i in range(n_ka - 1)])
    corner = lax.ppermute(
        below[tile_cols:],
        ("pb", "ka"),
        [(p * n_ka + a, (p + 1) * n_ka + a + 1) for p in range(n_pb - 1) for a in range(n_ka - 1)],
    )

    place = jnp.stack([pb_index * tile_rows, ka_index * tile_cols]).astype(jnp.int32)
    n_block = 2
    scale = math.log2(math.e) / math.sqrt(channels)
    states = pl.pallas_call(
        functools.partial(
            attention_kernel, tile_rows, float(row_count), float(col_count), scale
        ),
        grid=(n_pb // n_block,),
        in_specs=[
            pl.BlockSpec(memory_space=pltpu.SMEM),
            pl.BlockSpec((n_block, n_query + TAIL, channels), lambda i: (i, 0, 0)),
            whole(keys.shape),
            whole(top.shape),
            whole(left.shape),
            whole(above.shape),
            whole(side.shape),
            whole(corner.shape),
        ],
        out_specs=pl.BlockSpec((n_block, 4, n_query), lambda i: (i, 0, 0)),
        out_shape=jax.ShapeDtypeStruct((n_pb, 4, n_query), F32),
        scratch_shapes=[
            pltpu.VMEM(keys.shape, BF16),
            pltpu.VMEM((8, channels), F32),
            pltpu.VMEM((channels, n_block * n_query), BF16),
        ],
        compiler_params=params,
        name="attention",
    )(place, queries, keys, top, left, above, side, corner)

    mine = merged(lax.all_to_all(states, "pb", 0, 0))
    final = merged(lax.all_to_all(jnp.broadcast_to(mine[None], (n_ka, 4, n_query)), "ka", 0, 0))
    mean_x = (final[2] / final[1]).reshape(band_rows, band_cols)
    mean_y = (final[3] / final[1]).reshape(band_rows, band_cols)
    query_x = (
        2.0 * (pb_index * band_cols + jnp.arange(band_cols, dtype=jnp.int32)).astype(F32) + 1.0
    ) / col_count - 1.0
    band_top = (row_count - band_rows) // 2
    query_y = (
        2.0 * (band_top + jnp.arange(band_rows, dtype=jnp.int32)).astype(F32) + 1.0
    ) / row_count - 1.0
    return jnp.stack([mean_x - query_x[None, :], mean_y - query_y[:, None]])


def solution(mesh):
    in_specs = (P(None, "pb", "ka"), P(None, None, "pb"), P())
    out_specs = P(None, None, "pb")
    return jax.shard_map(
        on_device, mesh=mesh, in_specs=in_specs, out_specs=out_specs, check_vma=False
    )
```

time: 592 us -> 266 us (0.45)
  the two profiles are of different devices: /device:TPU:44 before, /device:TPU:1 now
where the time goes in v1:
time: 266 us; the launch traced here: 265 us
  Pallas kernels  174 us (65%)
  waiting for transfers between devices  51.6 us (19%)
  starting transfers between devices  22.7 us (9%)
  between operations  13.5 us (5%)
    pallas_call x1, Pallas kernels, on_device(): pl.pallas_call(functools.partial(attention_kernel, tile_rows, float(row_c...  161 us
    all_gather x1, waiting for transfers between devices, on_device(): queries = lax.all_gather(queries, 'pb')  35.4 us
    pallas_call x1, Pallas kernels, on_device(): pl.pallas_call(key_kernel, out_shape=(jax.ShapeDtypeStruct((n_key, channe...  11.5 us
    all_to_all x1, waiting for transfers between devices, on_device(): mine = merged(lax.all_to_all(states, 'pb', 0, 0))  10.8 us
    ppermute x1, starting transfers between devices, on_device(): above = lax.ppermute(below, 'pb', [(i, i + 1) for i in range(n_pb - 1)])  6.27 us
    all_to_all x1, starting transfers between devices, on_device(): mine = merged(lax.all_to_all(states, 'pb', 0, 0))  5.7 us
  transfers between devices with their start and end apart: 6, of which 4 were waited for; matrix products, arithmetic and copies ran while one was open for 1% of the time, Pallas kernels for 4%

profile of v1, /device:TPU:1, one launch (start us, length us, event | category | flops | bytes accessed | tf_op | source)
XLA Modules:
  0.0 265.2 jit_solution(6840606421667595808)
XLA Ops:
  6.5 0.0 all-gather.3.cloned.1.call-start
  6.5 2.2 query_feats.1
  8.8 0.0 all-gather.3.cloned.1.call-update
  8.8 11.5 %key_feats.1 = (bf16[4096,128]{1,0:T(8,128)(2,1)}, f32[256,128]{1,0:T(8,128)}, f32[16,8,128]{2,1,0:T(8,128)}, f32[264,128]{1,0:T(8,128)}, f32[16,128]{1,0:T(8,128)}) custom-call(bf16[96,32,512]{2,1,0:T(8,128)(2,1)} %x_ref.1, bf16[9,96,128]{2,1,0:T(8,128)(2,1)} %bitcast.14), custom_call_target="tpu_custom_call" | custom-call | tf_op jit(solution)/shard_map/key_feats/pallas_call | solution.py:271
  20.3 6.3 %collective-permute-start = (f32[264,128]{1,0:T(8,128)}, f32[264,128]{1,0:T(8,128)S(1)}, u32[]{:S(2)}, u32[]{:S(2)}) collective-permute-start(f32[264,128]{1,0:T(8,128)} %get-tuple-element.13), channel_id=1, source_target_pairs={{0,8},{8,16},{16,24},{24,32},{32,40},{40,48},{48,56},{56,64},{64,7... | collective-permute-start | bytes 405512 | tf_op jit(solution)/shard_map/ppermute | solution.py:286
  26.5 0.7 slice.27
  27.2 2.9 %collective-permute-start.2 = (f32[8,128]{1,0:T(8,128)S(1)}, f32[8,128]{1,0:T(8,128)S(1)}, u32[]{:S(2)}, u32[]{:S(2)}) collective-permute-start(f32[8,128]{1,0:T(8,128)S(1)} %slice.27), channel_id=1, source_target_pairs={{0,9},{1,10},{2,11},{3,12},{4,13},{5,14},{6,15},{8,17},{9,18},{10,... | collective-permute-start | bytes 12296 | tf_op jit(solution)/shard_map/ppermute | solution.py:288
  30.2 3.2 %collective-permute-start.1 = (f32[16,128]{1,0:T(8,128)}, f32[16,128]{1,0:T(8,128)S(1)}, u32[]{:S(2)}, u32[]{:S(2)}) collective-permute-start(f32[16,128]{1,0:T(8,128)} %get-tuple-element.14), channel_id=1, source_target_pairs={{0,1},{1,2},{2,3},{3,4},{4,5},{5,6},{6,7},{8,9},{9,10},{10,11},{11... | collective-permute-start | bytes 24584 | tf_op jit(solution)/shard_map/ppermute | solution.py:287
  33.4 0.6 pad_add_fusion.place_ref
  34.0 0.0 collective-permute-done.2.corner_ref
  34.0 0.0 copy-start.2
  34.0 0.3 collective-permute-done.1.side_ref
  34.4 0.0 copy-start.1
  34.4 0.0 collective-permute-done.above_ref
  34.4 0.0 copy-start
  34.4 35.4 %all-gather.3.cloned.1.call-done = bf16[9216,128]{1,0:T(8,128)(2,1)} async-done(((bf16[288,128]{1,0:T(8,128)(2,1)}), bf16[9216,128]{1,0:T(8,128)(2,1)}) %all-gather.3.cloned.1.call-update) | async-done | bytes 2359312 | tf_op jit(solution)/shard_map/all_gather | solution.py:268
  69.8 0.0 copy-done.2
  69.8 0.0 copy-done.1
  69.8 0.0 copy-done
  69.8 160.6 %attention.1 = f32[32,4,256]{2,1,0:T(4,128)} custom-call(s32[2]{0:T(128)} %pad_add_fusion.place_ref, bf16[32,288,128]{2,1,0:T(8,128)(2,1)} %bitcast.12, bf16[4096,128]{1,0:T(8,128)(2,1)} %get-tuple-element.10.key_ref, f32[256,128]{1,0:T(8,128)} %get-tuple-element.11.top_ref, f32[16,8,128]{2,1,0:T(8,128)} %get-tuple-element.12.left_ref, f32[264,128]{1,0:T(8,128)} %copy-done, ...), custom_call_target="tpu_custom_call" | custom-call | tf_op jit(solution)/shard_map/attention/pallas_call | solution.py:297
  230.4 5.7 %all-to-all-start = ((f32[32,4,256]{2,1,0:T(4,128)}), f32[32,4,256]{2,1,0:T(4,128)S(1)}, u32[]{:S(2)}, u32[]{:S(2)}) async-start(f32[32,4,256]{2,1,0:T(4,128)} %attention.1), calls=%async_computation | async-start | bytes 262144 | tf_op jit(solution)/shard_map/all_to_all | solution.py:323
  236.1 10.8 %all-to-all-done = f32[32,4,256]{2,1,0:T(4,128)S(1)} async-done(((f32[32,4,256]{2,1,0:T(4,128)}), f32[32,4,256]{2,1,0:T(4,128)S(1)}, u32[]{:S(2)}, u32[]{:S(2)}) %all-to-all-start) | async-done | bytes 131104 | tf_op jit(solution)/shard_map/all_to_all | solution.py:323
  246.9 0.1 slice_reduce_fusion
  247.0 0.1 multiply_exponential_fusion
  247.0 0.1 fusion
  247.1 0.6 broadcast_in_dim.5
  247.7 4.6 %all-to-all-start.1 = ((f32[8,4,256]{2,1,0:T(4,128)}), f32[8,4,256]{2,1,0:T(4,128)S(1)}, u32[]{:S(2)}, u32[]{:S(2)}) async-start(f32[8,4,256]{2,1,0:T(4,128)} %broadcast_in_dim.5), calls=%async_computation.1 | async-start | bytes 65536 | tf_op jit(solution)/shard_map/all_to_all | solution.py:324
  252.3 5.1 %all-to-all-done.1 = f32[8,4,256]{2,1,0:T(4,128)S(1)} async-done(((f32[8,4,256]{2,1,0:T(4,128)}), f32[8,4,256]{2,1,0:T(4,128)S(1)}, u32[]{:S(2)}, u32[]{:S(2)}) %all-to-all-start.1) | async-done | bytes 32800 | tf_op jit(solution)/shard_map/all_to_all | solution.py:324
  257.6 0.1 div.38
  257.6 0.1 div.42
  257.7 0.1 broadcast_subtract_fusion
  257.8 0.6 pad_maximum_fusion.1
  (9 shorter events, 0.1 us)
Async XLA Ops:
  6.5 63.2 %all-gather.3.cloned.1.call-start = ((), (), s32[]{:S(2)}) async-start(), calls=%async_computation.2 | async-start | bytes 2433024 | tf_op jit(solution)/shard_map/all_gather | solution.py:268
  20.3 14.1 %collective-permute-start = (f32[264,128]{1,0:T(8,128)}, f32[264,128]{1,0:T(8,128)S(1)}, u32[]{:S(2)}, u32[]{:S(2)}) collective-permute-start(f32[264,128]{1,0:T(8,128)} %get-tuple-element.13), channel_id=1, source_target_pairs={{0,8},{8,16},{16,24},{24,32},{32,40},{40,48},{48,56},{56,64},{64,7... | collective-permute-start | bytes 405512 | tf_op jit(solution)/shard_map/ppermute | solution.py:286
  27.2 6.8 %collective-permute-start.2 = (f32[8,128]{1,0:T(8,128)S(1)}, f32[8,128]{1,0:T(8,128)S(1)}, u32[]{:S(2)}, u32[]{:S(2)}) collective-permute-start(f32[8,128]{1,0:T(8,128)S(1)} %slice.27), channel_id=1, source_target_pairs={{0,9},{1,10},{2,11},{3,12},{4,13},{5,14},{6,15},{8,17},{9,18},{10,... | collective-permute-start | bytes 12296 | tf_op jit(solution)/shard_map/ppermute | solution.py:288
  30.2 4.2 %collective-permute-start.1 = (f32[16,128]{1,0:T(8,128)}, f32[16,128]{1,0:T(8,128)S(1)}, u32[]{:S(2)}, u32[]{:S(2)}) collective-permute-start(f32[16,128]{1,0:T(8,128)} %get-tuple-element.14), channel_id=1, source_target_pairs={{0,1},{1,2},{2,3},{3,4},{4,5},{5,6},{6,7},{8,9},{9,10},{10,11},{11... | collective-permute-start | bytes 24584 | tf_op jit(solution)/shard_map/ppermute | solution.py:287
  34.0 35.7 %copy-start.2 = (f32[8,128]{1,0:T(8,128)}, f32[8,128]{1,0:T(8,128)S(1)}, u32[]{:S(2)}) copy-start(f32[8,128]{1,0:T(8,128)S(1)} %collective-permute-done.2.corner_ref) | copy-start | bytes 12292
  34.4 35.4 %copy-start.1 = (f32[16,128]{1,0:T(8,128)}, f32[16,128]{1,0:T(8,128)S(1)}, u32[]{:S(2)}) copy-start(f32[16,128]{1,0:T(8,128)S(1)} %collective-permute-done.1.side_ref) | copy-start | bytes 24580
  34.4 35.4 %copy-start = (f32[264,128]{1,0:T(8,128)}, f32[264,128]{1,0:T(8,128)S(1)}, u32[]{:S(2)}) copy-start(f32[264,128]{1,0:T(8,128)S(1)} %collective-permute-done.above_ref) | copy-start | bytes 405508
  230.4 16.5 %all-to-all-start = ((f32[32,4,256]{2,1,0:T(4,128)}), f32[32,4,256]{2,1,0:T(4,128)S(1)}, u32[]{:S(2)}, u32[]{:S(2)}) async-start(f32[32,4,256]{2,1,0:T(4,128)} %attention.1), calls=%async_computation | async-start | bytes 262144 | tf_op jit(solution)/shard_map/all_to_all | solution.py:323
  247.7 9.7 %all-to-all-start.1 = ((f32[8,4,256]{2,1,0:T(4,128)}), f32[8,4,256]{2,1,0:T(4,128)S(1)}, u32[]{:S(2)}, u32[]{:S(2)}) async-start(f32[8,4,256]{2,1,0:T(4,128)} %broadcast_in_dim.5), calls=%async_computation.1 | async-start | bytes 65536 | tf_op jit(solution)/shard_map/all_to_all | solution.py:324
Sparse Core Ops, SparseCore 0:
  9.9 59.8 all-gather.2

commit v2 on v1

v2 whole, which is shorter than its diff:
```python
import functools
import math

import jax
import jax.numpy as jnp
from jax import lax
from jax.experimental import pallas as pl
from jax.experimental.pallas import tpu as pltpu
from jax.sharding import PartitionSpec as P

BF16 = jnp.bfloat16
F32 = jnp.float32
GROUP = 8
VMEM = 56 * 1024 * 1024


def dot(a, b):
    return jnp.dot(a, b, preferred_element_type=F32)


def dot_nt(a, b):
    return lax.dot_general(a, b, (((1,), (1,)), ((), ())), preferred_element_type=F32)


def iota(shape, axis):
    return lax.broadcasted_iota(jnp.int32, shape, axis)


def tap_selector(cols):
    half = cols // 2
    row = iota((3 * half, cols), 0)
    tap = row // half
    source = 2 * (row - tap * half) - 1 + tap
    return (iota((3 * half, cols), 1) == source).astype(BF16)


def split3(x):
    high = x.astype(BF16)
    rest = x - high.astype(F32)
    mid = rest.astype(BF16)
    low = (rest - mid.astype(F32)).astype(BF16)
    return high, mid, low


def query_kernel(band_ref, w_ref, out_ref, edge_ref):
    rows_in, _, cols = band_ref.shape
    rows = (rows_in - 1) // 2
    half = cols // 2
    n_query = rows * half
    channels = w_ref.shape[2]
    selector = tap_selector(cols)
    picked = [dot_nt(selector, band_ref[r]).astype(BF16) for r in range(rows_in)]
    total = jnp.zeros((n_query, channels), F32)
    beyond = jnp.zeros((rows * 16, channels), F32)
    for a in range(3):
        for b in range(3):
            lhs = jnp.concatenate(
                [picked[2 * r + a][b * half : (b + 1) * half] for r in range(rows)], axis=0
            )
            total = total + dot(lhs, w_ref[3 * a + b])
        last = jnp.concatenate(
            [picked[2 * r + a][3 * half - 16 : 3 * half] for r in range(rows)], axis=0
        )
        beyond = beyond + dot(last, w_ref[3 * a])
    out_ref[...] = total.astype(BF16)
    edge_ref[...] = jnp.concatenate(
        [total[r * half : r * half + 1] for r in range(rows)]
        + [beyond[r * 16 + 15 : r * 16 + 16] for r in range(rows)],
        axis=0,
    )


def spread_kernel(main_ref, edge_ref, before_ref, out_ref):
    n_query = main_ref.shape[0]
    rows = edge_ref.shape[0] // 2
    half = n_query // rows
    fixed = edge_ref[0:rows, :] + before_ref[rows:, :]
    pieces = []
    for r in range(rows):
        old = main_ref[r * half : r * half + 16, :].astype(F32)
        new = jnp.where(
            iota(old.shape, 0) == 0, jnp.broadcast_to(fixed[r : r + 1], old.shape), old
        )
        pieces += [new.astype(BF16), main_ref[r * half + 16 : (r + 1) * half, :]]
    full = jnp.concatenate(pieces, axis=0)
    for i in range(out_ref.shape[0]):
        out_ref[i] = full


def key_kernel(x_ref, w_ref, key_ref, top_ref, left_ref, below_ref, right_ref, band_ref):
    channels_in, rows_in, cols = x_ref.shape
    half = cols // 2
    channels = w_ref.shape[2]
    depth = channels_in * GROUP
    outs = GROUP // 2
    n_group = rows_in // GROUP
    expand = (iota((depth, channels_in), 0) // GROUP == iota((depth, channels_in), 1)).astype(BF16)
    row = iota((depth, channels), 0) % GROUP
    for b in range(3):
        spread = [dot(expand, w_ref[3 * a + b]) for a in range(3)]
        for i in range(outs + 1):
            block = jnp.zeros((depth, channels), F32)
            for a in range(3):
                block = jnp.where(row == 2 * i - 1 + a, spread[a], block)
            band_ref[b, :, i * channels : (i + 1) * channels] = block.astype(BF16)
    selector = tap_selector(cols)
    carried = jnp.zeros((half, channels), F32)
    carried_right = jnp.zeros((1, channels), F32)
    for g in range(n_group):
        base = (g * GROUP) // 16 * 16
        pair = x_ref[:, base : base + 16, :].astype(F32)
        off = g * GROUP - base
        x = pair[:, off : off + GROUP, :].reshape(depth, cols).astype(BF16)
        picked = dot_nt(selector, x).astype(BF16)
        total = dot(picked[0:half], band_ref[0])
        total = total + dot(picked[half : 2 * half], band_ref[1])
        total = total + dot(picked[2 * half : 3 * half], band_ref[2])
        beyond = dot(picked[3 * half - 16 : 3 * half], band_ref[0])
        for i in range(outs):
            part = total[:, i * channels : (i + 1) * channels]
            part_right = beyond[15:16, i * channels : (i + 1) * channels]
            if i == 0:
                part = part + carried
                part_right = part_right + carried_right
            o = g * outs + i
            key_ref[o * half : (o + 1) * half, :] = part.astype(BF16)
            left_ref[o] = part[0:8]
            right_ref[o : o + 1, :] = part_right
            if o == 0:
                top_ref[...] = part
        carried = total[:, outs * channels :]
        carried_right = beyond[15:16, outs * channels :]
    below_ref[0:half, :] = carried
    below_ref[half:, :] = jnp.broadcast_to(carried_right, (8, channels))


def bit_tree(leaf, start, count):
    if count == 1:
        return leaf(start), []
    low, low_bits = bit_tree(leaf, start, count // 2)
    high, high_bits = bit_tree(leaf, start + count // 2, count // 2)
    return low + high, [a + b for a, b in zip(low_bits, high_bits)] + [high]


def attention_kernel(
    tile_rows, row_count, col_count, scale, second,
    place_ref, query_ref, key_ref, top_ref, left_ref, above_ref, side_ref, corner_ref, *refs,
):
    if second:
        other_ref, out_ref, keys, qt, acc = refs
    else:
        out_ref, keys, qt, acc = refs
    n_block, n_query, channels = query_ref.shape
    tile_cols = key_ref.shape[0] // tile_rows
    groups = tile_cols // 8
    n_bits = int(math.log2(groups))
    width = n_block * n_query
    chunk = min(width, 512)
    depth = keys.shape[1]

    @pl.when(pl.program_id(0) == 0)
    def _():
        pad = (keys.shape[0], depth - channels)
        keys[:, 0:channels] = key_ref[...]
        keys[:, channels:] = jnp.where(iota(pad, 1) < 3, -1.0, 0.0).astype(BF16)
        top = top_ref[...] + above_ref[0:tile_cols, :]
        first = jnp.broadcast_to(side_ref[0:1, :] + corner_ref[0:1, :], top.shape)
        top = jnp.where(iota(top.shape, 0) == 0, top + first, top)
        keys[0:tile_cols, 0:channels] = top.astype(BF16)
        for i in range(1, tile_rows):
            edge = left_ref[i][0:1, :] + side_ref[i : i + 1, :]
            rows = slice(i * tile_cols, i * tile_cols + 16)
            old = keys[rows, 0:channels].astype(F32)
            new = jnp.where(iota(old.shape, 0) == 0, jnp.broadcast_to(edge, old.shape), old)
            keys[rows, 0:channels] = new.astype(BF16)

    def set_shift(shift):
        parts = split3(shift) + (jnp.zeros((depth - channels - 3, width), BF16),)
        qt[channels:, :] = jnp.concatenate([v.astype(F32) for v in parts], axis=0).astype(BF16)

    for p in range(n_block):
        qt[0:channels, p * n_query : (p + 1) * n_query] = query_ref[p].T

    def add_row(i, start):
        for h in range(width // chunk):
            scores = dot(keys[pl.ds(start, tile_cols), :], qt[:, h * chunk : (h + 1) * chunk])
            for l in range(chunk // 128):
                lanes = slice(h * chunk + l * 128, h * chunk + (l + 1) * 128)

                def leaf(g):
                    return jnp.exp2(scores[8 * g : 8 * g + 8, l * 128 : (l + 1) * 128] * scale)

                total, bits = bit_tree(leaf, 0, groups)
                for n, v in enumerate([total, i * total] + bits):
                    acc[n, :, lanes] += v

    def write(shift):
        total, down = acc[0], acc[1]
        along = sum(float(2**b) * acc[2 + b] for b in range(n_bits))
        sub = iota(total.shape, 0).astype(F32)
        first_row = place_ref[0].astype(F32)
        first_col = place_ref[1].astype(F32)
        x = ((2.0 * (first_col + sub) + 1.0) / col_count - 1.0) * total + (16.0 / col_count) * along
        y = ((2.0 * first_row + 1.0) / row_count - 1.0) * total + (2.0 / row_count) * down
        parts = [shift] + [jnp.sum(v, axis=0, keepdims=True) for v in (total, x, y)]
        for p in range(n_block):
            lanes = slice(p * n_query, (p + 1) * n_query)
            block = jnp.concatenate([v[:, lanes] for v in parts], axis=0)
            if second:
                out_ref[p, 1 - place_ref[2]] = block
                out_ref[p, place_ref[2]] = other_ref[p]
            else:
                out_ref[p] = block

    sample = jnp.concatenate(
        [keys[i * tile_cols : i * tile_cols + 16, 0:channels] for i in range(tile_rows)], axis=0
    )
    shift = jnp.max(dot(sample, qt[0:channels, :]), axis=0, keepdims=True)
    set_shift(shift)
    acc[...] = jnp.zeros_like(acc)
    for i in range(tile_rows):
        add_row(float(i), i * tile_cols)
    write(shift)

    @pl.when(jnp.logical_not(jnp.max(acc[0]) < 1e30))
    def _():
        def raise_max(i, top):
            start = pl.multiple_of(i * tile_cols, tile_cols)
            scores = dot(keys[pl.ds(start, tile_cols), 0:channels], qt[0:channels, :])
            return jnp.maximum(top, jnp.max(scores, axis=0, keepdims=True))

        top = lax.fori_loop(0, tile_rows, raise_max, jnp.full((1, width), -jnp.inf, F32))
        set_shift(top)
        acc[...] = jnp.zeros_like(acc)

        def again(i, carry):
            add_row(i.astype(F32), pl.multiple_of(i * tile_cols, tile_cols))
            return carry

        lax.fori_loop(0, tile_rows, again, 0)
        write(top)


def whole(shape):
    return pl.BlockSpec(shape, lambda *_: (0,) * len(shape))


def merged(states, scale):
    highest = jnp.max(states[:, 0], axis=0)
    factor = jnp.exp2((states[:, 0] - highest[None]) * scale)
    sums = jnp.sum(states[:, 1:] * factor[:, None], axis=0)
    return jnp.concatenate([highest[None], sums], axis=0)


def on_device(frame_two, frame_band, conv_weight):
    channels_in, rows_in, cols_in = frame_two.shape
    channels = conv_weight.shape[1]
    tile_rows, tile_cols = rows_in // 2, cols_in // 2
    band_rows, band_cols = (frame_band.shape[1] - 1) // 2, frame_band.shape[2] // 2
    pb = ("chip", "core")
    n_chip, n_pb, n_ka = lax.axis_size("chip"), lax.axis_size(pb), lax.axis_size("ka")
    row_count, col_count = tile_rows * n_pb, tile_cols * n_ka
    pb_index, ka_index = lax.axis_index(pb), lax.axis_index("ka")
    n_query = band_rows * band_cols
    weights = conv_weight.transpose(0, 2, 1)
    params = pltpu.CompilerParams(vmem_limit_bytes=VMEM)

    main, edge = pl.pallas_call(
        query_kernel,
        out_shape=(
            jax.ShapeDtypeStruct((n_query, channels), BF16),
            jax.ShapeDtypeStruct((2 * band_rows, channels), F32),
        ),
        compiler_params=params,
        name="query_feats",
    )(frame_band.transpose(1, 0, 2), weights)
    before = lax.ppermute(edge, pb, [(i, i + 1) for i in range(n_pb - 1)])
    copies = pl.pallas_call(
        spread_kernel,
        out_shape=jax.ShapeDtypeStruct((n_chip, n_query, channels), BF16),
        compiler_params=params,
        name="query_copies",
    )(main, edge, before)
    queries = lax.all_to_all(copies, "chip", 0, 0)

    n_key = tile_rows * tile_cols
    keys, top, left, below, right = pl.pallas_call(
        key_kernel,
        out_shape=(
            jax.ShapeDtypeStruct((n_key, channels), BF16),
            jax.ShapeDtypeStruct((tile_cols, channels), F32),
            jax.ShapeDtypeStruct((tile_rows, 8, channels), F32),
            jax.ShapeDtypeStruct((tile_cols + 8, channels), F32),
            jax.ShapeDtypeStruct((tile_rows, channels), F32),
        ),
        scratch_shapes=[
            pltpu.VMEM((3, channels_in * GROUP, (GROUP // 2 + 1) * channels), BF16)
        ],
        compiler_params=params,
        name="key_feats",
    )(frame_two, weights)
    above = lax.ppermute(below, pb, [(i, i + 1) for i in range(n_pb - 1)])
    side = lax.ppermute(right, "ka", [(i, i + 1) for i in range(n_ka - 1)])
    corner = lax.ppermute(
        below[tile_cols:],
        ("chip", "core", "ka"),
        [(p * n_ka + a, (p + 1) * n_ka + a + 1) for p in range(n_pb - 1) for a in range(n_ka - 1)],
    )
    queries, above, side, corner = lax.optimization_barrier((queries, above, side, corner))
    twins = lax.ppermute(queries, "core", [(0, 1), (1, 0)])

    place = jnp.stack(
        [pb_index * tile_rows, ka_index * tile_cols, lax.axis_index("core")]
    ).astype(jnp.int32)
    n_block = 4
    scale = math.log2(math.e) / math.sqrt(channels)

    def attend(block, other):
        ins = [keys, top, left, above, side, corner]
        in_specs = [
            pl.BlockSpec(memory_space=pltpu.SMEM),
            pl.BlockSpec((n_block, n_query, channels), lambda i: (i, 0, 0)),
        ] + [whole(v.shape) for v in ins]
        if other is None:
            out_spec = pl.BlockSpec((n_block, 4, n_query), lambda i: (i, 0, 0))
            out_shape = (n_chip, 4, n_query)
        else:
            ins.append(other)
            in_specs.append(pl.BlockSpec((n_block, 4, n_query), lambda i: (i, 0, 0)))
            out_spec = pl.BlockSpec((n_block, 2, 4, n_query), lambda i: (i, 0, 0, 0))
            out_shape = (n_chip, 2, 4, n_query)
        return pl.pallas_call(
            functools.partial(
                attention_kernel,
                tile_rows, float(row_count), float(col_count), scale, other is not None,
            ),
            grid=(n_chip // n_block,),
            in_specs=in_specs,
            out_specs=out_spec,
            out_shape=jax.ShapeDtypeStruct(out_shape, F32),
            scratch_shapes=[
                pltpu.VMEM((n_key, channels + 16), BF16),
                pltpu.VMEM((channels + 16, n_block * n_query), BF16),
                pltpu.VMEM((2 + int(math.log2(tile_cols // 8)), 8, n_block * n_query), F32),
            ],
            compiler_params=params,
            name="attention",
        )(place, block, *ins)

    states = attend(twins, attend(queries, None)).reshape(n_pb, 4, n_query)
    mine = merged(lax.all_to_all(states, pb, 0, 0), scale)
    copies = jnp.broadcast_to(mine[None], (n_ka, 4, n_query))
    final = merged(lax.all_to_all(copies, "ka", 0, 0), scale)
    mean_x = (final[2] / final[1]).reshape(band_rows, band_cols)
    mean_y = (final[3] / final[1]).reshape(band_rows, band_cols)
    query_x = (
        2.0 * (pb_index * band_cols + jnp.arange(band_cols, dtype=jnp.int32)).astype(F32) + 1.0
    ) / col_count - 1.0
    band_top = (row_count - band_rows) // 2
    query_y = (
        2.0 * (band_top + jnp.arange(band_rows, dtype=jnp.int32)).astype(F32) + 1.0
    ) / row_count - 1.0
    return jnp.stack([mean_x - query_x[None, :], mean_y - query_y[:, None]])


def solution(mesh):
    n_pb, n_ka = mesh.shape["pb"], mesh.shape["ka"]
    finer = jax.sharding.Mesh(
        mesh.devices.reshape(n_pb // 2, 2, n_ka), ("chip", "core", "ka")
    )
    pb = ("chip", "core")
    in_specs = (P(None, pb, "ka"), P(None, None, pb), P())
    out_specs = P(None, None, pb)
    return jax.shard_map(
        on_device, mesh=finer, in_specs=in_specs, out_specs=out_specs, check_vma=False
    )
```

time: 266 us -> 202 us (0.76)
  Pallas kernels: 174 us -> 133 us
  waiting for transfers between devices: 51.6 us -> 17.5 us
  starting transfers between devices: 22.7 us -> 46.1 us
  between operations: 13.5 us -> 0.13 us
    pallas_call x2 -> x4, Pallas kernels: 163 us -> 122 us  [the longest x2 117 us: attend(): pl.pallas_call(functools.partial(attention_kernel, tile_rows, float(row_c...]
    all_gather x1 -> x0, waiting for transfers between devices: 35.4 us -> none  [on_device(): queries = lax.all_gather(queries, 'pb')]
    ppermute x2 -> x4, starting transfers between devices: 9.19 us -> 24.3 us  [the longest x1 7.9 us: on_device(): above = lax.ppermute(below, pb, [(i, i + 1) for i in range(n_pb - 1)])]
    all_to_all x2 -> x3, starting transfers between devices: 10.3 us -> 18.6 us  [the longest x1 8.97 us: on_device(): queries = lax.all_to_all(copies, 'chip', 0, 0)]
    all_to_all x2 -> x3, waiting for transfers between devices: 15.9 us -> 15.8 us  [the longest x1 10.7 us: on_device(): mine = merged(lax.all_to_all(states, pb, 0, 0), scale)]
  transfers between devices with their start and end apart: 6 -> 8, of which waited for: 4 -> 4; matrix products, arithmetic and copies ran while one was open for 1% -> 1% of each run, Pallas kernels for 4% -> 35%
where the time goes in v2:
time: 202 us; the launch traced here: 201 us
  Pallas kernels  133 us (66%)
  starting transfers between devices  46.1 us (23%)
  waiting for transfers between devices  17.5 us (9%)
  local copies, waits for them, and re-layouts  3.07 us (2%)
    pallas_call x2, Pallas kernels, attend(): pl.pallas_call(functools.partial(attention_kernel, tile_rows, float(row_c...  117 us
    pallas_call x1, Pallas kernels, on_device(): pl.pallas_call(key_kernel, out_shape=(jax.ShapeDtypeStruct((n_key, channe...  11.5 us
    all_to_all x1, waiting for transfers between devices, on_device(): mine = merged(lax.all_to_all(states, pb, 0, 0), scale)  10.7 us
    all_to_all x1, starting transfers between devices, on_device(): queries = lax.all_to_all(copies, 'chip', 0, 0)  8.97 us
    ppermute x1, starting transfers between devices, on_device(): above = lax.ppermute(below, pb, [(i, i + 1) for i in range(n_pb - 1)])  7.9 us
    ppermute x1, starting transfers between devices, on_device(): twins = lax.ppermute(queries, 'core', [(0, 1), (1, 0)])  6.94 us
    ppermute x1, starting transfers between devices, on_device(): before = lax.ppermute(edge, pb, [(i, i + 1) for i in range(n_pb - 1)])  6.25 us
    all_to_all x1, starting transfers between devices, on_device(): final = merged(lax.all_to_all(copies, 'ka', 0, 0), scale)  5.77 us
  transfers between devices with their start and end apart: 8, of which 4 were waited for; matrix products, arithmetic and copies ran while one was open for 1% of the time, Pallas kernels for 35%

profile of v2, /device:TPU:1, one launch (start us, length us, event | category | flops | bytes accessed | tf_op | source)
XLA Modules:
  0.0 201.5 jit_solution(14043347751431160040)
XLA Ops:
  0.0 2.2 %query_feats.1 = (bf16[256,128]{1,0:T(8,128)(2,1)}, f32[8,128]{1,0:T(8,128)}) custom-call(bf16[9,96,128]{2,1,0:T(8,128)(2,1)} %bitcast.16, bf16[9,96,128]{2,1,0:T(8,128)(2,1)} %bitcast.13), custom_call_target="tpu_custom_call" | custom-call | tf_op jit(solution)/shard_map/query_feats/pallas_call | solution.py:268
  2.2 6.3 %collective-permute-start = (f32[8,128]{1,0:T(8,128)}, f32[8,128]{1,0:T(8,128)S(1)}, u32[]{:S(2)}, u32[]{:S(2)}) collective-permute-start(f32[8,128]{1,0:T(8,128)} %get-tuple-element.17.edge_ref), channel_id=1, source_target_pairs={{0,8},{8,16},{16,24},{24,32},{32,40},{40,48},{48,56},{56,64},{64,7... | collective-permute-start | bytes 12296 | tf_op jit(solution)/shard_map/ppermute | solution.py:277
  8.5 0.9 collective-permute-done.before_ref
  9.4 0.0 copy-start.5
  9.4 0.6 copy-done.5
  10.0 2.0 %query_copies.1 = bf16[16,256,128]{2,1,0:T(8,128)(2,1)} custom-call(bf16[256,128]{1,0:T(8,128)(2,1)} %get-tuple-element.16.main_ref, f32[8,128]{1,0:T(8,128)} %get-tuple-element.17.edge_ref, f32[8,128]{1,0:T(8,128)} %copy-done.5), custom_call_target="tpu_custom_call" | custom-call | tf_op jit(solution)/shard_map/query_copies/pallas_call | solution.py:278
  12.1 9.0 %all-to-all-start = ((bf16[16,256,128]{2,1,0:T(8,128)(2,1)}), bf16[16,256,128]{2,1,0:T(8,128)(2,1)S(1)}, u32[]{:S(2)}, u32[]{:S(2)}) async-start(bf16[16,256,128]{2,1,0:T(8,128)(2,1)} %query_copies.1), calls=%async_computation | async-start | bytes 2097152 | tf_op jit(solution)/shard_map/all_to_all | solution.py:284
  21.0 11.5 %key_feats.1 = (bf16[4096,128]{1,0:T(8,128)(2,1)}, f32[256,128]{1,0:T(8,128)}, f32[16,8,128]{2,1,0:T(8,128)}, f32[264,128]{1,0:T(8,128)}, f32[16,128]{1,0:T(8,128)}) custom-call(bf16[96,32,512]{2,1,0:T(8,128)(2,1)} %x_ref.1, bf16[9,96,128]{2,1,0:T(8,128)(2,1)} %bitcast.14), custom_call_target="tpu_custom_call" | custom-call | tf_op jit(solution)/shard_map/key_feats/pallas_call | solution.py:287
  32.5 7.9 %collective-permute-start.1 = (f32[264,128]{1,0:T(8,128)}, f32[264,128]{1,0:T(8,128)S(1)}, u32[]{:S(2)}, u32[]{:S(2)}) collective-permute-start(f32[264,128]{1,0:T(8,128)} %get-tuple-element.18), channel_id=1, source_target_pairs={{0,8},{8,16},{16,24},{24,32},{32,40},{40,48},{48,56},{56,64},{64,7... | collective-permute-start | bytes 405512 | tf_op jit(solution)/shard_map/ppermute | solution.py:302
  40.4 3.2 %collective-permute-start.2 = (f32[16,128]{1,0:T(8,128)}, f32[16,128]{1,0:T(8,128)S(1)}, u32[]{:S(2)}, u32[]{:S(2)}) collective-permute-start(f32[16,128]{1,0:T(8,128)} %get-tuple-element.19), channel_id=1, source_target_pairs={{0,1},{1,2},{2,3},{3,4},{4,5},{5,6},{6,7},{8,9},{9,10},{10,11},{11... | collective-permute-start | bytes 24584 | tf_op jit(solution)/shard_map/ppermute | solution.py:303
  43.6 0.7 slice.27
  44.3 3.2 %collective-permute-start.3 = (f32[8,128]{1,0:T(8,128)S(1)}, f32[8,128]{1,0:T(8,128)S(1)}, u32[]{:S(2)}, u32[]{:S(2)}) collective-permute-start(f32[8,128]{1,0:T(8,128)S(1)} %slice.27), channel_id=1, source_target_pairs={{0,9},{1,10},{2,11},{3,12},{4,13},{5,14},{6,15},{8,17},{9,18},{10,... | collective-permute-start | bytes 12296 | tf_op jit(solution)/shard_map/ppermute | solution.py:304
  47.5 0.7 collective-permute-done.3.corner_ref
  48.2 0.0 copy-start.4
  48.2 0.0 collective-permute-done.2.side_ref
  48.2 0.0 copy-start.3
  48.2 0.0 collective-permute-done.1.above_ref
  48.3 0.0 copy-start.2
  48.3 0.0 all-to-all-done.query_ref
  48.3 0.0 copy-start
  48.3 6.9 %collective-permute-start.4 = (bf16[16,256,128]{2,1,0:T(8,128)(2,1)S(1)}, bf16[16,256,128]{2,1,0:T(8,128)(2,1)S(1)}, u32[]{:S(2)}, u32[]{:S(2)}) collective-permute-start(bf16[16,256,128]{2,1,0:T(8,128)(2,1)S(1)} %all-to-all-done.query_ref), channel_id=1, source_target_pairs={{0,8},{8,0},{1,9},{9,1},{2,10},{10,2},{3,11},{11,3},{4,12},{12,4},... | collective-permute-start | bytes 3145736 | tf_op jit(solution)/shard_map/ppermute | solution.py:310
  55.2 0.7 pad_add_fusion.place_ref
  55.9 0.0 copy-done.4
  55.9 0.0 copy-done.3
  55.9 0.0 copy-done.2
  55.9 0.0 copy-done
  55.9 58.6 %attention.2.refs_0_ = f32[16,4,256]{2,1,0:T(4,128)} custom-call(s32[3]{0:T(128)} %pad_add_fusion.place_ref, bf16[16,256,128]{2,1,0:T(8,128)(2,1)} %copy-done, bf16[4096,128]{1,0:T(8,128)(2,1)} %get-tuple-element.21.key_ref, f32[256,128]{1,0:T(8,128)} %get-tuple-element.22.top_ref, f32[16,8,128]{2,1,0:T(8,128)} %get-tuple-element.23.left_ref, ...), custom_call_target="tpu_custom_call" | custom-call | tf_op jit(solution)/shard_map/attention/pallas_call | solution.py:332
  114.5 0.0 collective-permute-done.4.query_ref
  114.5 0.0 copy-start.1
  114.5 1.0 copy-done.1
  115.6 58.7 %attention.3 = f32[16,2,4,256]{3,2,1,0:T(4,128)} custom-call(s32[3]{0:T(128)} %pad_add_fusion.place_ref, bf16[16,256,128]{2,1,0:T(8,128)(2,1)} %copy-done.1, bf16[4096,128]{1,0:T(8,128)(2,1)} %get-tuple-element.21.key_ref, f32[256,128]{1,0:T(8,128)} %get-tuple-element.22.top_ref, f32[16,8,128]{2,1,0:T(8,128)} %get-tuple-element.23.left_ref, ...), custom_call_target="tpu_custom_call" | custom-call | tf_op jit(solution)/shard_map/attention/pallas_call | solution.py:332
  174.2 3.8 %all-to-all-start.1 = ((f32[32,4,256]{2,1,0:T(4,128)}), f32[32,4,256]{2,1,0:T(4,128)S(1)}, u32[]{:S(2)}, u32[]{:S(2)}) async-start(f32[32,4,256]{2,1,0:T(4,128)} %bitcast.15), calls=%async_computation.1 | async-start | bytes 262144 | tf_op jit(solution)/shard_map/all_to_all | solution.py:351
  178.1 10.7 %all-to-all-done.1 = f32[32,4,256]{2,1,0:T(4,128)S(1)} async-done(((f32[32,4,256]{2,1,0:T(4,128)}), f32[32,4,256]{2,1,0:T(4,128)S(1)}, u32[]{:S(2)}, u32[]{:S(2)}) %all-to-all-start.1) | async-done | bytes 131104 | tf_op jit(solution)/shard_map/all_to_all | solution.py:351
  188.8 0.1 slice_reduce_fusion
  188.9 0.1 multiply_exponential_fusion
  189.0 0.1 fusion
  189.0 0.6 broadcast_in_dim.5
  189.6 5.8 %all-to-all-start.2 = ((f32[8,4,256]{2,1,0:T(4,128)}), f32[8,4,256]{2,1,0:T(4,128)S(1)}, u32[]{:S(2)}, u32[]{:S(2)}) async-start(f32[8,4,256]{2,1,0:T(4,128)} %broadcast_in_dim.5), calls=%async_computation.2 | async-start | bytes 65536 | tf_op jit(solution)/shard_map/all_to_all | solution.py:353
  195.4 5.1 %all-to-all-done.2 = f32[8,4,256]{2,1,0:T(4,128)S(1)} async-done(((f32[8,4,256]{2,1,0:T(4,128)}), f32[8,4,256]{2,1,0:T(4,128)S(1)}, u32[]{:S(2)}, u32[]{:S(2)}) %all-to-all-start.2) | async-done | bytes 32800 | tf_op jit(solution)/shard_map/all_to_all | solution.py:353
  200.6 0.1 div.42
  200.7 0.1 div.38
  200.8 0.1 broadcast_subtract_fusion
  200.9 0.6 pad_maximum_fusion.1
  (9 shorter events, 0.1 us)
Async XLA Ops:
  2.2 7.2 %collective-permute-start = (f32[8,128]{1,0:T(8,128)}, f32[8,128]{1,0:T(8,128)S(1)}, u32[]{:S(2)}, u32[]{:S(2)}) collective-permute-start(f32[8,128]{1,0:T(8,128)} %get-tuple-element.17.edge_ref), channel_id=1, source_target_pairs={{0,8},{8,16},{16,24},{24,32},{32,40},{40,48},{48,56},{56,64},{64,7... | collective-permute-start | bytes 12296 | tf_op jit(solution)/shard_map/ppermute | solution.py:277
  9.4 0.6 copy-start.5
  12.1 36.2 %all-to-all-start = ((bf16[16,256,128]{2,1,0:T(8,128)(2,1)}), bf16[16,256,128]{2,1,0:T(8,128)(2,1)S(1)}, u32[]{:S(2)}, u32[]{:S(2)}) async-start(bf16[16,256,128]{2,1,0:T(8,128)(2,1)} %query_copies.1), calls=%async_computation | async-start | bytes 2097152 | tf_op jit(solution)/shard_map/all_to_all | solution.py:284
  32.5 15.7 %collective-permute-start.1 = (f32[264,128]{1,0:T(8,128)}, f32[264,128]{1,0:T(8,128)S(1)}, u32[]{:S(2)}, u32[]{:S(2)}) collective-permute-start(f32[264,128]{1,0:T(8,128)} %get-tuple-element.18), channel_id=1, source_target_pairs={{0,8},{8,16},{16,24},{24,32},{32,40},{40,48},{48,56},{56,64},{64,7... | collective-permute-start | bytes 405512 | tf_op jit(solution)/shard_map/ppermute | solution.py:302
  40.4 7.8 %collective-permute-start.2 = (f32[16,128]{1,0:T(8,128)}, f32[16,128]{1,0:T(8,128)S(1)}, u32[]{:S(2)}, u32[]{:S(2)}) collective-permute-start(f32[16,128]{1,0:T(8,128)} %get-tuple-element.19), channel_id=1, source_target_pairs={{0,1},{1,2},{2,3},{3,4},{4,5},{5,6},{6,7},{8,9},{9,10},{10,11},{11... | collective-permute-start | bytes 24584 | tf_op jit(solution)/shard_map/ppermute | solution.py:303
  44.3 3.9 %collective-permute-start.3 = (f32[8,128]{1,0:T(8,128)S(1)}, f32[8,128]{1,0:T(8,128)S(1)}, u32[]{:S(2)}, u32[]{:S(2)}) collective-permute-start(f32[8,128]{1,0:T(8,128)S(1)} %slice.27), channel_id=1, source_target_pairs={{0,9},{1,10},{2,11},{3,12},{4,13},{5,14},{6,15},{8,17},{9,18},{10,... | collective-permute-start | bytes 12296 | tf_op jit(solution)/shard_map/ppermute | solution.py:304
  48.2 7.6 %copy-start.4 = (f32[8,128]{1,0:T(8,128)}, f32[8,128]{1,0:T(8,128)S(1)}, u32[]{:S(2)}) copy-start(f32[8,128]{1,0:T(8,128)S(1)} %collective-permute-done.3.corner_ref) | copy-start | bytes 12292
  48.2 7.6 %copy-start.3 = (f32[16,128]{1,0:T(8,128)}, f32[16,128]{1,0:T(8,128)S(1)}, u32[]{:S(2)}) copy-start(f32[16,128]{1,0:T(8,128)S(1)} %collective-permute-done.2.side_ref) | copy-start | bytes 24580
  48.3 7.6 %copy-start.2 = (f32[264,128]{1,0:T(8,128)}, f32[264,128]{1,0:T(8,128)S(1)}, u32[]{:S(2)}) copy-start(f32[264,128]{1,0:T(8,128)S(1)} %collective-permute-done.1.above_ref) | copy-start | bytes 405508
  48.3 7.6 %copy-start = (bf16[16,256,128]{2,1,0:T(8,128)(2,1)}, bf16[16,256,128]{2,1,0:T(8,128)(2,1)S(1)}, u32[]{:S(2)}) copy-start(bf16[16,256,128]{2,1,0:T(8,128)(2,1)S(1)} %all-to-all-done.query_ref) | copy-start | bytes 3145732
  48.3 66.3 %collective-permute-start.4 = (bf16[16,256,128]{2,1,0:T(8,128)(2,1)S(1)}, bf16[16,256,128]{2,1,0:T(8,128)(2,1)S(1)}, u32[]{:S(2)}, u32[]{:S(2)}) collective-permute-start(bf16[16,256,128]{2,1,0:T(8,128)(2,1)S(1)} %all-to-all-done.query_ref), channel_id=1, source_target_pairs={{0,8},{8,0},{1,9},{9,1},{2,10},{10,2},{3,11},{11,3},{4,12},{12,4},... | collective-permute-start | bytes 3145736 | tf_op jit(solution)/shard_map/ppermute | solution.py:310
  114.5 1.0 copy-start.1
  174.2 14.6 %all-to-all-start.1 = ((f32[32,4,256]{2,1,0:T(4,128)}), f32[32,4,256]{2,1,0:T(4,128)S(1)}, u32[]{:S(2)}, u32[]{:S(2)}) async-start(f32[32,4,256]{2,1,0:T(4,128)} %bitcast.15), calls=%async_computation.1 | async-start | bytes 262144 | tf_op jit(solution)/shard_map/all_to_all | solution.py:351
  189.6 10.9 %all-to-all-start.2 = ((f32[8,4,256]{2,1,0:T(4,128)}), f32[8,4,256]{2,1,0:T(4,128)S(1)}, u32[]{:S(2)}, u32[]{:S(2)}) async-start(f32[8,4,256]{2,1,0:T(4,128)} %broadcast_in_dim.5), calls=%async_computation.2 | async-start | bytes 65536 | tf_op jit(solution)/shard_map/all_to_all | solution.py:353

commit v3 on v2

--- a/solution.py
+++ b/solution.py
@@ -42,8 +42,22 @@
     return high, mid, low
 
 
-def query_kernel(band_ref, w_ref, out_ref, edge_ref):
-    rows_in, _, cols = band_ref.shape
+def last_lane(x):
+    rows, cols = x.shape
+    picker = (iota((16, cols), 1) == cols - 1).astype(BF16)
+    return dot_nt(picker, x)
+
+
+def group_of(x_ref, g):
+    channels_in, _, cols = x_ref.shape
+    base = (g * GROUP) // 16 * 16
+    pair = x_ref[:, base : base + 16, :].astype(F32)
+    off = g * GROUP - base
+    return pair[:, off : off + GROUP, :].reshape(channels_in * GROUP, cols).astype(BF16)
+
+
+def query_kernel(band_ref, w_ref, bottom_ref, right_ref, out_ref, edge_ref, down_ref, side_ref):
+    rows_in, channels_in, cols = band_ref.shape
     rows = (rows_in - 1) // 2
     half = cols // 2
     n_query = rows * half
@@ -64,17 +78,40 @@
         beyond = beyond + dot(last, w_ref[3 * a])
     out_ref[...] = total.astype(BF16)
     edge_ref[...] = jnp.concatenate(
-        [total[r * half : r * half + 1] for r in range(rows)]
-        + [beyond[r * 16 + 15 : r * 16 + 16] for r in range(rows)],
+        [total[r * half : r * half + 1] for r in range(rows)] * 2, axis=0
+    )
+
+    depth = channels_in * GROUP
+    wide = bottom_ref.shape[2]
+    picker = (iota((channels_in, depth), 1) == iota((channels_in, depth), 0) * GROUP + GROUP - 1)
+    last_group = bottom_ref.shape[1] // GROUP - 1
+    bottom = dot(picker.astype(BF16), group_of(bottom_ref, last_group))
+    down_ref[0:channels_in, :] = bottom.astype(BF16)
+    ext = jnp.concatenate(
+        [beyond[r * 16 + 15 : r * 16 + 16] for r in range(rows)]
+        + [jnp.zeros((16 - rows, channels), F32)],
         axis=0,
     )
-
-
-def spread_kernel(main_ref, edge_ref, before_ref, out_ref):
-    n_query = main_ref.shape[0]
+    parts = [v.astype(F32) for v in split3(ext)]
+    blank = jnp.zeros((16, wide - 3 * channels), F32)
+    down_ref[channels_in:, :] = jnp.concatenate(parts + [blank], axis=1).astype(BF16)
+
+    side = jnp.zeros((16, depth), F32)
+    for g in range(right_ref.shape[1] // GROUP):
+        side = jnp.where(iota(side.shape, 0) == g, last_lane(group_of(right_ref, g)), side)
+    side_ref[...] = side.astype(BF16)
+
+
+def spread_kernel(main_ref, edge_ref, down_ref, side_ref, out_ref, corner_ref):
+    n_query, channels = main_ref.shape
     rows = edge_ref.shape[0] // 2
     half = n_query // rows
-    fixed = edge_ref[0:rows, :] + before_ref[rows:, :]
+    depth = side_ref.shape[1]
+    channels_in = depth // GROUP
+    wide = down_ref.shape[1]
+    tail = down_ref[channels_in:, :].astype(F32)
+    before = sum(tail[:, n * channels : (n + 1) * channels] for n in range(3))
+    fixed = edge_ref[...] + before[0:8]
     pieces = []
     for r in range(rows):
         old = main_ref[r * half : r * half + 16, :].astype(F32)
@@ -85,9 +122,13 @@
     full = jnp.concatenate(pieces, axis=0)
     for i in range(out_ref.shape[0]):
         out_ref[i] = full
-
-
-def key_kernel(x_ref, w_ref, key_ref, top_ref, left_ref, below_ref, right_ref, band_ref):
+    row = down_ref[0:channels_in, wide - 128 :]
+    row = jnp.concatenate([row, jnp.zeros((depth - channels_in, 128), BF16)], axis=0)
+    side = side_ref[...].astype(F32)
+    corner_ref[...] = jnp.where(iota(side.shape, 0) == 8, last_lane(row), side).astype(BF16)
+
+
+def key_kernel(x_ref, w_ref, above_ref, side_ref, key_ref, band_ref):
     channels_in, rows_in, cols = x_ref.shape
     half = cols // 2
     channels = w_ref.shape[2]
@@ -104,34 +145,28 @@
                 block = jnp.where(row == 2 * i - 1 + a, spread[a], block)
             band_ref[b, :, i * channels : (i + 1) * channels] = block.astype(BF16)
     selector = tap_selector(cols)
-    carried = jnp.zeros((half, channels), F32)
-    carried_right = jnp.zeros((1, channels), F32)
+    side = side_ref[...].astype(F32)
+
+    def taps(x, left):
+        picked = dot_nt(selector, x)
+        first = picked[0:half]
+        first = jnp.where(iota(first.shape, 0) == 0, jnp.broadcast_to(left, first.shape), first)
+        return first.astype(BF16), picked[half : 2 * half].astype(BF16), picked[2 * half :].astype(BF16)
+
+    upper = taps(above_ref[0:channels_in, :], side[8:9, 0:channels_in])
+    carried = sum(dot(upper[b], w_ref[b]) for b in range(3))
     for g in range(n_group):
-        base = (g * GROUP) // 16 * 16
-        pair = x_ref[:, base : base + 16, :].astype(F32)
-        off = g * GROUP - base
-        x = pair[:, off : off + GROUP, :].reshape(depth, cols).astype(BF16)
-        picked = dot_nt(selector, x).astype(BF16)
-        total = dot(picked[0:half], band_ref[0])
-        total = total + dot(picked[half : 2 * half], band_ref[1])
-        total = total + dot(picked[2 * half : 3 * half], band_ref[2])
-        beyond = dot(picked[3 * half - 16 : 3 * half], band_ref[0])
+        picked = taps(group_of(x_ref, g), side[g : g + 1])
+        total = sum(dot(picked[b], band_ref[b]) for b in range(3))
         for i in range(outs):
             part = total[:, i * channels : (i + 1) * channels]
-            part_right = beyond[15:16, i * channels : (i + 1) * channels]
             if i == 0:
                 part = part + carried
-                part_right = part_right + carried_right
             o = g * outs + i
-            key_ref[o * half : (o + 1) * half, :] = part.astype(BF16)
-            left_ref[o] = part[0:8]
-            right_ref[o : o + 1, :] = part_right
-            if o == 0:
-                top_ref[...] = part
+            key_ref[o * half : (o + 1) * half, 0:channels] = part.astype(BF16)
         carried = total[:, outs * channels :]
-        carried_right = beyond[15:16, outs * channels :]
-    below_ref[0:half, :] = carried
-    below_ref[half:, :] = jnp.broadcast_to(carried_right, (8, channels))
+    pad = (key_ref.shape[0], key_ref.shape[1] - channels)
+    key_ref[:, channels:] = jnp.where(iota(pad, 1) < 3, -1.0, 0.0).astype(BF16)
 
 
 def bit_tree(leaf, start, count):
@@ -144,35 +179,19 @@
 
 def attention_kernel(
     tile_rows, row_count, col_count, scale, second,
-    place_ref, query_ref, key_ref, top_ref, left_ref, above_ref, side_ref, corner_ref, *refs,
+    place_ref, query_ref, keys, *refs,
 ):
     if second:
-        other_ref, out_ref, keys, qt, acc = refs
+        other_ref, out_ref, qt, acc = refs
     else:
-        out_ref, keys, qt, acc = refs
+        out_ref, qt, acc = refs
     n_block, n_query, channels = query_ref.shape
-    tile_cols = key_ref.shape[0] // tile_rows
+    tile_cols = keys.shape[0] // tile_rows
     groups = tile_cols // 8
     n_bits = int(math.log2(groups))
     width = n_block * n_query
     chunk = min(width, 512)
     depth = keys.shape[1]
-
-    @pl.when(pl.program_id(0) == 0)
-    def _():
-        pad = (keys.shape[0], depth - channels)
-        keys[:, 0:channels] = key_ref[...]
-        keys[:, channels:] = jnp.where(iota(pad, 1) < 3, -1.0, 0.0).astype(BF16)
-        top = top_ref[...] + above_ref[0:tile_cols, :]
-        first = jnp.broadcast_to(side_ref[0:1, :] + corner_ref[0:1, :], top.shape)
-        top = jnp.where(iota(top.shape, 0) == 0, top + first, top)
-        keys[0:tile_cols, 0:channels] = top.astype(BF16)
-        for i in range(1, tile_rows):
-            edge = left_ref[i][0:1, :] + side_ref[i : i + 1, :]
-            rows = slice(i * tile_cols, i * tile_cols + 16)
-            old = keys[rows, 0:channels].astype(F32)
-            new = jnp.where(iota(old.shape, 0) == 0, jnp.broadcast_to(edge, old.shape), old)
-            keys[rows, 0:channels] = new.astype(BF16)
 
     def set_shift(shift):
         parts = split3(shift) + (jnp.zeros((depth - channels - 3, width), BF16),)
@@ -265,48 +284,47 @@
     weights = conv_weight.transpose(0, 2, 1)
     params = pltpu.CompilerParams(vmem_limit_bytes=VMEM)
 
-    main, edge = pl.pallas_call(
+    depth = channels_in * GROUP
+    whole_band = (band_rows * 2 + 1, channels_in, 2 * band_cols)
+    outs = (
+        jax.ShapeDtypeStruct((n_query, channels), BF16),
+        jax.ShapeDtypeStruct((2 * band_rows, channels), F32),
+        jax.ShapeDtypeStruct((channels_in + 16, cols_in), BF16),
+        jax.ShapeDtypeStruct((16, depth), BF16),
+    )
+    main, edge, down, right = pl.pallas_call(
         query_kernel,
-        out_shape=(
-            jax.ShapeDtypeStruct((n_query, channels), BF16),
-            jax.ShapeDtypeStruct((2 * band_rows, channels), F32),
-        ),
+        grid=(1,),
+        in_specs=[
+            whole(whole_band),
+            whole(weights.shape),
+            pl.BlockSpec((channels_in, 16, cols_in), lambda i: (0, rows_in // 16 - 1, 0)),
+            pl.BlockSpec((channels_in, rows_in, 128), lambda i: (0, 0, cols_in // 128 - 1)),
+        ],
+        out_specs=[whole(v.shape) for v in outs],
+        out_shape=outs,
         compiler_params=params,
         name="query_feats",
-    )(frame_band.transpose(1, 0, 2), weights)
-    before = lax.ppermute(edge, pb, [(i, i + 1) for i in range(n_pb - 1)])
-    copies = pl.pallas_call(
+    )(frame_band.transpose(1, 0, 2), weights, frame_two, frame_two)
+    above = lax.ppermute(down, pb, [(i, i + 1) for i in range(n_pb - 1)])
+    copies, right = pl.pallas_call(
         spread_kernel,
-        out_shape=jax.ShapeDtypeStruct((n_chip, n_query, channels), BF16),
+        out_shape=(jax.ShapeDtypeStruct((n_chip, n_query, channels), BF16), outs[3]),
         compiler_params=params,
         name="query_copies",
-    )(main, edge, before)
+    )(main, edge, above, right)
+    side = lax.ppermute(right, "ka", [(i, i + 1) for i in range(n_ka - 1)])
     queries = lax.all_to_all(copies, "chip", 0, 0)
 
     n_key = tile_rows * tile_cols
-    keys, top, left, below, right = pl.pallas_call(
+    keys = pl.pallas_call(
         key_kernel,
-        out_shape=(
-            jax.ShapeDtypeStruct((n_key, channels), BF16),
-            jax.ShapeDtypeStruct((tile_cols, channels), F32),
-            jax.ShapeDtypeStruct((tile_rows, 8, channels), F32),
-            jax.ShapeDtypeStruct((tile_cols + 8, channels), F32),
-            jax.ShapeDtypeStruct((tile_rows, channels), F32),
-        ),
-        scratch_shapes=[
-            pltpu.VMEM((3, channels_in * GROUP, (GROUP // 2 + 1) * channels), BF16)
-        ],
+        out_shape=jax.ShapeDtypeStruct((n_key, channels + 16), BF16),
+        scratch_shapes=[pltpu.VMEM((3, depth, (GROUP // 2 + 1) * channels), BF16)],
         compiler_params=params,
         name="key_feats",
-    )(frame_two, weights)
-    above = lax.ppermute(below, pb, [(i, i + 1) for i in range(n_pb - 1)])
-    side = lax.ppermute(right, "ka", [(i, i + 1) for i in range(n_ka - 1)])
-    corner = lax.ppermute(
-        below[tile_cols:],
-        ("chip", "core", "ka"),
-        [(p * n_ka + a, (p + 1) * n_ka + a + 1) for p in range(n_pb - 1) for a in range(n_ka - 1)],
-    )
-    queries, above, side, corner = lax.optimization_barrier((queries, above, side, corner))
+    )(frame_two, weights, above, side)
+    queries, keys = lax.optimization_barrier((queries, keys))
     twins = lax.ppermute(queries, "core", [(0, 1), (1, 0)])
 
     place = jnp.stack(
@@ -316,7 +334,7 @@
     scale = math.log2(math.e) / math.sqrt(channels)
 
     def attend(block, other):
-        ins = [keys, top, left, above, side, corner]
+        ins = [keys]
         in_specs = [
             pl.BlockSpec(memory_space=pltpu.SMEM),
             pl.BlockSpec((n_block, n_query, channels), lambda i: (i, 0, 0)),
@@ -339,7 +357,6 @@
             out_specs=out_spec,
             out_shape=jax.ShapeDtypeStruct(out_shape, F32),
             scratch_shapes=[
-                pltpu.VMEM((n_key, channels + 16), BF16),
                 pltpu.VMEM((channels + 16, n_block * n_query), BF16),
                 pltpu.VMEM((2 + int(math.log2(tile_cols // 8)), 8, n_block * n_query), F32),
             ],

time: 202 us -> 212 us (1.050)
  waiting for transfers between devices: 17.5 us -> 25 us
    all_to_all x1, starting transfers between devices: 5.77 us -> 18.7 us  [on_device(): final = merged(lax.all_to_all(copies, 'ka', 0, 0), scale)]
    ppermute x3 -> x1, starting transfers between devices: 17.4 us -> 6.29 us  [on_device(): above = lax.ppermute(down, pb, [(i, i + 1) for i in range(n_pb - 1)])]
    all_to_all x1, waiting for transfers between devices: 0.01 us -> 6.08 us  [on_device(): queries = lax.all_to_all(copies, 'chip', 0, 0)]
    ppermute x1, starting transfers between devices: 6.94 us -> 3.18 us  [on_device(): twins = lax.ppermute(queries, 'core', [(0, 1), (1, 0)])]
    all_to_all x1, starting transfers between devices: 3.83 us -> 7.51 us  [on_device(): mine = merged(lax.all_to_all(states, pb, 0, 0), scale)]
  transfers between devices with their start and end apart: 8 -> 6, of which waited for: 4 -> 5; matrix products, arithmetic and copies ran while one was open for 1% -> 0% of each run, Pallas kernels for 35% -> 33%
where the time goes in v3:
time: 212 us
  Pallas kernels  134 us (63%)
  starting transfers between devices  47.8 us (23%)
  waiting for transfers between devices  25 us (12%)
  local copies, waits for them, and re-layouts  3.01 us (1%)
    pallas_call x2, Pallas kernels, attend(): pl.pallas_call(functools.partial(attention_kernel, tile_rows, float(row_c...  117 us
    all_to_all x1, starting transfers between devices, on_device(): final = merged(lax.all_to_all(copies, 'ka', 0, 0), scale)  18.7 us
    pallas_call x1, Pallas kernels, on_device(): pl.pallas_call(key_kernel, out_shape=jax.ShapeDtypeStruct((n_key, channel...  11.6 us
    all_to_all x1, waiting for transfers between devices, on_device(): mine = merged(lax.all_to_all(states, pb, 0, 0), scale)  10.6 us
    all_to_all x1, starting transfers between devices, on_device(): queries = lax.all_to_all(copies, 'chip', 0, 0)  8.94 us
    all_to_all x1, starting transfers between devices, on_device(): mine = merged(lax.all_to_all(states, pb, 0, 0), scale)  7.51 us
    ppermute x1, starting transfers between devices, on_device(): above = lax.ppermute(down, pb, [(i, i + 1) for i in range(n_pb - 1)])  6.29 us
    all_to_all x1, waiting for transfers between devices, on_device(): queries = lax.all_to_all(copies, 'chip', 0, 0)  6.08 us
  transfers between devices with their start and end apart: 6, of which 5 were waited for; matrix products, arithmetic and copies ran while one was open for 0% of the time, Pallas kernels for 33%

profile of v3, /device:TPU:1, one launch (start us, length us, event | category | flops | bytes accessed | tf_op | source)
XLA Modules:
  0.0 211.6 jit_solution(9628281533135277367)
XLA Ops:
  0.0 3.3 %query_feats.1 = (bf16[256,128]{1,0:T(8,128)(2,1)}, f32[8,128]{1,0:T(8,128)}, bf16[112,512]{1,0:T(8,128)(2,1)}, bf16[16,768]{1,0:T(8,128)(2,1)}) custom-call(bf16[9,96,128]{2,1,0:T(8,128)(2,1)} %bitcast.16, bf16[9,96,128]{2,1,0:T(8,128)(2,1)} %bitcast.13, bf16[96,32,512]{2,1,0:T(8,128)(2,1)} %x_ref.1, bf16[96,32,512]{2,1,0:T(8,128)(2,1)} %x_ref.1), custom_call_target="tpu_custom_call" | custom-call | tf_op jit(solution)/shard_map/query_feats/pallas_call | solution.py:295
  3.3 6.3 %collective-permute-start = (bf16[112,512]{1,0:T(8,128)(2,1)}, bf16[112,512]{1,0:T(8,128)(2,1)S(1)}, u32[]{:S(2)}, u32[]{:S(2)}) collective-permute-start(bf16[112,512]{1,0:T(8,128)(2,1)} %get-tuple-element.15), channel_id=1, source_target_pairs={{0,8},{8,16},{16,24},{24,32},{32,40},{40,48},{48,56},{56,64},{64,7... | collective-permute-start | bytes 344072 | tf_op jit(solution)/shard_map/ppermute | solution.py:309
  9.6 2.1 collective-permute-done.down_ref.above_ref
  11.7 0.0 copy-start.2
  11.7 0.6 copy-done.2
  12.3 2.1 query_copies.1
  14.4 8.9 %all-to-all-start = ((bf16[16,256,128]{2,1,0:T(8,128)(2,1)}), bf16[16,256,128]{2,1,0:T(8,128)(2,1)S(1)}, u32[]{:S(2)}, u32[]{:S(2)}) async-start(bf16[16,256,128]{2,1,0:T(8,128)(2,1)} %get-tuple-element.17), calls=%async_computation | async-start | bytes 2097152 | tf_op jit(solution)/shard_map/all_to_all | solution.py:317
  23.3 3.2 %collective-permute-start.1 = (bf16[16,768]{1,0:T(8,128)(2,1)}, bf16[16,768]{1,0:T(8,128)(2,1)S(1)}, u32[]{:S(2)}, u32[]{:S(2)}) collective-permute-start(bf16[16,768]{1,0:T(8,128)(2,1)} %get-tuple-element.18), channel_id=1, source_target_pairs={{0,1},{1,2},{2,3},{3,4},{4,5},{5,6},{6,7},{8,9},{9,10},{10,11},{11... | collective-permute-start | bytes 73736 | tf_op jit(solution)/shard_map/ppermute | solution.py:316
  26.6 1.1 collective-permute-done.1.side_ref
  27.7 0.0 copy-start.3
  27.7 0.6 copy-done.3
  28.3 11.6 %key_feats.1.keys = bf16[4096,144]{1,0:T(8,128)(2,1)} custom-call(bf16[96,32,512]{2,1,0:T(8,128)(2,1)} %x_ref.1, bf16[9,96,128]{2,1,0:T(8,128)(2,1)} %bitcast.14, bf16[112,512]{1,0:T(8,128)(2,1)} %copy-done.2, bf16[16,768]{1,0:T(8,128)(2,1)} %copy-done.3), custom_call_target="tpu_custom_call" | custom-call | tf_op jit(solution)/shard_map/key_feats/pallas_call | solution.py:320
  39.9 6.1 %all-to-all-done.query_ref = bf16[16,256,128]{2,1,0:T(8,128)(2,1)S(1)} async-done(((bf16[16,256,128]{2,1,0:T(8,128)(2,1)}), bf16[16,256,128]{2,1,0:T(8,128)(2,1)S(1)}, u32[]{:S(2)}, u32[]{:S(2)}) %all-to-all-start) | async-done | bytes 1048608 | tf_op jit(solution)/shard_map/all_to_all | solution.py:317
  46.0 0.0 copy-start
  46.0 3.2 %collective-permute-start.2 = (bf16[16,256,128]{2,1,0:T(8,128)(2,1)S(1)}, bf16[16,256,128]{2,1,0:T(8,128)(2,1)S(1)}, u32[]{:S(2)}, u32[]{:S(2)}) collective-permute-start(bf16[16,256,128]{2,1,0:T(8,128)(2,1)S(1)} %all-to-all-done.query_ref), channel_id=1, source_target_pairs={{0,8},{8,0},{1,9},{9,1},{2,10},{10,2},{3,11},{11,3},{4,12},{12,4},... | collective-permute-start | bytes 3145736 | tf_op jit(solution)/shard_map/ppermute | solution.py:328
  49.1 0.7 pad_add_fusion.place_ref
  49.8 0.0 copy-done
  49.8 58.5 %attention.2.refs_0_ = f32[16,4,256]{2,1,0:T(4,128)} custom-call(s32[3]{0:T(128)} %pad_add_fusion.place_ref, bf16[16,256,128]{2,1,0:T(8,128)(2,1)} %copy-done, bf16[4096,144]{1,0:T(8,128)(2,1)} %key_feats.1.keys), custom_call_target="tpu_custom_call" | custom-call | tf_op jit(solution)/shard_map/attention/pallas_call | solution.py:350
  108.3 0.0 collective-permute-done.2.query_ref
  108.3 0.0 copy-start.1
  108.3 1.0 copy-done.1
  109.3 58.6 %attention.3 = f32[16,2,4,256]{3,2,1,0:T(4,128)} custom-call(s32[3]{0:T(128)} %pad_add_fusion.place_ref, bf16[16,256,128]{2,1,0:T(8,128)(2,1)} %copy-done.1, bf16[4096,144]{1,0:T(8,128)(2,1)} %key_feats.1.keys, f32[16,4,256]{2,1,0:T(4,128)} %attention.2.refs_0_), custom_call_target="tpu_custom_call" | custom-call | tf_op jit(solution)/shard_map/attention/pallas_call | solution.py:350
  167.8 7.5 %all-to-all-start.1 = ((f32[32,4,256]{2,1,0:T(4,128)}), f32[32,4,256]{2,1,0:T(4,128)S(1)}, u32[]{:S(2)}, u32[]{:S(2)}) async-start(f32[32,4,256]{2,1,0:T(4,128)} %bitcast.15), calls=%async_computation.1 | async-start | bytes 262144 | tf_op jit(solution)/shard_map/all_to_all | solution.py:368
  175.4 10.6 %all-to-all-done.1 = f32[32,4,256]{2,1,0:T(4,128)S(1)} async-done(((f32[32,4,256]{2,1,0:T(4,128)}), f32[32,4,256]{2,1,0:T(4,128)S(1)}, u32[]{:S(2)}, u32[]{:S(2)}) %all-to-all-start.1) | async-done | bytes 131104 | tf_op jit(solution)/shard_map/all_to_all | solution.py:368
  186.0 0.1 slice_reduce_fusion
  186.1 0.1 multiply_exponential_fusion
  186.1 0.1 fusion
  186.2 0.6 broadcast_in_dim.5
  186.8 18.7 %all-to-all-start.2 = ((f32[8,4,256]{2,1,0:T(4,128)}), f32[8,4,256]{2,1,0:T(4,128)S(1)}, u32[]{:S(2)}, u32[]{:S(2)}) async-start(f32[8,4,256]{2,1,0:T(4,128)} %broadcast_in_dim.5), calls=%async_computation.2 | async-start | bytes 65536 | tf_op jit(solution)/shard_map/all_to_all | solution.py:370
  205.5 5.1 %all-to-all-done.2 = f32[8,4,256]{2,1,0:T(4,128)S(1)} async-done(((f32[8,4,256]{2,1,0:T(4,128)}), f32[8,4,256]{2,1,0:T(4,128)S(1)}, u32[]{:S(2)}, u32[]{:S(2)}) %all-to-all-start.2) | async-done | bytes 32800 | tf_op jit(solution)/shard_map/all_to_all | solution.py:370
  210.7 0.1 div.42
  210.8 0.1 div.38
  210.9 0.1 broadcast_subtract_fusion
  211.0 0.6 pad_maximum_fusion.1
  (9 shorter events, 0.1 us)
Async XLA Ops:
  3.3 8.4 %collective-permute-start = (bf16[112,512]{1,0:T(8,128)(2,1)}, bf16[112,512]{1,0:T(8,128)(2,1)S(1)}, u32[]{:S(2)}, u32[]{:S(2)}) collective-permute-start(bf16[112,512]{1,0:T(8,128)(2,1)} %get-tuple-element.15), channel_id=1, source_target_pairs={{0,8},{8,16},{16,24},{24,32},{32,40},{40,48},{48,56},{56,64},{64,7... | collective-permute-start | bytes 344072 | tf_op jit(solution)/shard_map/ppermute | solution.py:309
  11.7 0.6 copy-start.2
  14.4 31.6 %all-to-all-start = ((bf16[16,256,128]{2,1,0:T(8,128)(2,1)}), bf16[16,256,128]{2,1,0:T(8,128)(2,1)S(1)}, u32[]{:S(2)}, u32[]{:S(2)}) async-start(bf16[16,256,128]{2,1,0:T(8,128)(2,1)} %get-tuple-element.17), calls=%async_computation | async-start | bytes 2097152 | tf_op jit(solution)/shard_map/all_to_all | solution.py:317
  23.3 4.4 %collective-permute-start.1 = (bf16[16,768]{1,0:T(8,128)(2,1)}, bf16[16,768]{1,0:T(8,128)(2,1)S(1)}, u32[]{:S(2)}, u32[]{:S(2)}) collective-permute-start(bf16[16,768]{1,0:T(8,128)(2,1)} %get-tuple-element.18), channel_id=1, source_target_pairs={{0,1},{1,2},{2,3},{3,4},{4,5},{5,6},{6,7},{8,9},{9,10},{10,11},{11... | collective-permute-start | bytes 73736 | tf_op jit(solution)/shard_map/ppermute | solution.py:316
  27.7 0.6 copy-start.3
  46.0 3.8 %copy-start = (bf16[16,256,128]{2,1,0:T(8,128)(2,1)}, bf16[16,256,128]{2,1,0:T(8,128)(2,1)S(1)}, u32[]{:S(2)}) copy-start(bf16[16,256,128]{2,1,0:T(8,128)(2,1)S(1)} %all-to-all-done.query_ref) | copy-start | bytes 3145732
  46.0 62.3 %collective-permute-start.2 = (bf16[16,256,128]{2,1,0:T(8,128)(2,1)S(1)}, bf16[16,256,128]{2,1,0:T(8,128)(2,1)S(1)}, u32[]{:S(2)}, u32[]{:S(2)}) collective-permute-start(bf16[16,256,128]{2,1,0:T(8,128)(2,1)S(1)} %all-to-all-done.query_ref), channel_id=1, source_target_pairs={{0,8},{8,0},{1,9},{9,1},{2,10},{10,2},{3,11},{11,3},{4,12},{12,4},... | collective-permute-start | bytes 3145736 | tf_op jit(solution)/shard_map/ppermute | solution.py:328
  108.3 1.0 copy-start.1
  167.8 18.2 %all-to-all-start.1 = ((f32[32,4,256]{2,1,0:T(4,128)}), f32[32,4,256]{2,1,0:T(4,128)S(1)}, u32[]{:S(2)}, u32[]{:S(2)}) async-start(f32[32,4,256]{2,1,0:T(4,128)} %bitcast.15), calls=%async_computation.1 | async-start | bytes 262144 | tf_op jit(solution)/shard_map/all_to_all | solution.py:368
  186.8 23.8 %all-to-all-start.2 = ((f32[8,4,256]{2,1,0:T(4,128)}), f32[8,4,256]{2,1,0:T(4,128)S(1)}, u32[]{:S(2)}, u32[]{:S(2)}) async-start(f32[8,4,256]{2,1,0:T(4,128)} %broadcast_in_dim.5), calls=%async_computation.2 | async-start | bytes 65536 | tf_op jit(solution)/shard_map/all_to_all | solution.py:370

commit v4 on v3

--- a/solution.py
+++ b/solution.py
@@ -314,6 +314,7 @@
         name="query_copies",
     )(main, edge, above, right)
     side = lax.ppermute(right, "ka", [(i, i + 1) for i in range(n_ka - 1)])
+    copies, side = lax.optimization_barrier((copies, side))
     queries = lax.all_to_all(copies, "chip", 0, 0)
 
     n_key = tile_rows * tile_cols

time: 212 us -> 205 us (0.967)
  starting transfers between devices: 47.8 us -> 37.5 us
  waiting for transfers between devices: 25 us -> 29 us
    all_to_all x1, starting transfers between devices: 18.7 us -> 6.99 us  [on_device(): final = merged(lax.all_to_all(copies, 'ka', 0, 0), scale)]
    all_to_all x1, waiting for transfers between devices: 6.08 us -> 10.1 us  [on_device(): queries = lax.all_to_all(copies, 'chip', 0, 0)]
  transfers between devices with their start and end apart: 6 -> 6, of which waited for: 5 -> 5; matrix products, arithmetic and copies ran while one was open for 0% -> 0% of each run, Pallas kernels for 33% -> 34%
where the time goes in v4:
time: 205 us
  Pallas kernels  134 us (65%)
  starting transfers between devices  37.5 us (18%)
  waiting for transfers between devices  29 us (14%)
  local copies, waits for them, and re-layouts  2.42 us (1%)
    pallas_call x2, Pallas kernels, attend(): pl.pallas_call(functools.partial(attention_kernel, tile_rows, float(row_c...  117 us
    pallas_call x1, Pallas kernels, on_device(): pl.pallas_call(key_kernel, out_shape=jax.ShapeDtypeStruct((n_key, channel...  11.6 us
    all_to_all x1, waiting for transfers between devices, on_device(): mine = merged(lax.all_to_all(states, pb, 0, 0), scale)  10.6 us
    all_to_all x1, waiting for transfers between devices, on_device(): queries = lax.all_to_all(copies, 'chip', 0, 0)  10.1 us
    all_to_all x1, starting transfers between devices, on_device(): queries = lax.all_to_all(copies, 'chip', 0, 0)  8.95 us
    all_to_all x1, starting transfers between devices, on_device(): mine = merged(lax.all_to_all(states, pb, 0, 0), scale)  8 us
    all_to_all x1, starting transfers between devices, on_device(): final = merged(lax.all_to_all(copies, 'ka', 0, 0), scale)  6.99 us
    ppermute x1, starting transfers between devices, on_device(): above = lax.ppermute(down, pb, [(i, i + 1) for i in range(n_pb - 1)])  6.29 us
  transfers between devices with their start and end apart: 6, of which 5 were waited for; matrix products, arithmetic and copies ran while one was open for 0% of the time, Pallas kernels for 34%

profile of v4, /device:TPU:1, one launch (start us, length us, event | category | flops | bytes accessed | tf_op | source)
XLA Modules:
  0.0 204.7 jit_solution(5693463954008513859)
XLA Ops:
  0.0 3.3 %query_feats.1 = (bf16[256,128]{1,0:T(8,128)(2,1)}, f32[8,128]{1,0:T(8,128)}, bf16[112,512]{1,0:T(8,128)(2,1)}, bf16[16,768]{1,0:T(8,128)(2,1)}) custom-call(bf16[9,96,128]{2,1,0:T(8,128)(2,1)} %bitcast.16, bf16[9,96,128]{2,1,0:T(8,128)(2,1)} %bitcast.13, bf16[96,32,512]{2,1,0:T(8,128)(2,1)} %x_ref.1, bf16[96,32,512]{2,1,0:T(8,128)(2,1)} %x_ref.1), custom_call_target="tpu_custom_call" | custom-call | tf_op jit(solution)/shard_map/query_feats/pallas_call | solution.py:295
  3.3 6.3 %collective-permute-start = (bf16[112,512]{1,0:T(8,128)(2,1)}, bf16[112,512]{1,0:T(8,128)(2,1)S(1)}, u32[]{:S(2)}, u32[]{:S(2)}) collective-permute-start(bf16[112,512]{1,0:T(8,128)(2,1)} %get-tuple-element.17), channel_id=1, source_target_pairs={{0,8},{8,16},{16,24},{24,32},{32,40},{40,48},{48,56},{56,64},{64,7... | collective-permute-start | bytes 344072 | tf_op jit(solution)/shard_map/ppermute | solution.py:309
  9.6 2.1 %collective-permute-done.down_ref.above_ref = bf16[112,512]{1,0:T(8,128)(2,1)S(1)} collective-permute-done((bf16[112,512]{1,0:T(8,128)(2,1)}, bf16[112,512]{1,0:T(8,128)(2,1)S(1)}, u32[]{:S(2)}, u32[]{:S(2)}) %collective-permute-start) | collective-permute-done | bytes 114720 | tf_op jit(solution)/shard_map/ppermute | solution.py:309
  11.7 0.0 copy-start.2
  11.7 0.6 copy-done.2
  12.3 2.1 %query_copies.1 = (bf16[16,256,128]{2,1,0:T(8,128)(2,1)}, bf16[16,768]{1,0:T(8,128)(2,1)}) custom-call(bf16[256,128]{1,0:T(8,128)(2,1)} %get-tuple-element.15.main_ref, f32[8,128]{1,0:T(8,128)} %get-tuple-element.16.edge_ref, bf16[112,512]{1,0:T(8,128)(2,1)} %copy-done.2, bf16[16,768]{1,0:T(8,128)(2,1)} %get-tuple-element.18.side_ref), custom_call_target="tpu_custom_call" | custom-call | tf_op jit(solution)/shard_map/query_copies/pallas_call | solution.py:310
  14.4 3.2 %collective-permute-start.1 = (bf16[16,768]{1,0:T(8,128)(2,1)}, bf16[16,768]{1,0:T(8,128)(2,1)S(1)}, u32[]{:S(2)}, u32[]{:S(2)}) collective-permute-start(bf16[16,768]{1,0:T(8,128)(2,1)} %get-tuple-element.20), channel_id=1, source_target_pairs={{0,1},{1,2},{2,3},{3,4},{4,5},{5,6},{6,7},{8,9},{9,10},{10,11},{11... | collective-permute-start | bytes 73736 | tf_op jit(solution)/shard_map/ppermute | solution.py:316
  17.6 1.1 collective-permute-done.1.side_ref
  18.7 0.0 copy-start.3
  18.7 8.9 %all-to-all-start = ((bf16[16,256,128]{2,1,0:T(8,128)(2,1)}), bf16[16,256,128]{2,1,0:T(8,128)(2,1)S(1)}, u32[]{:S(2)}, u32[]{:S(2)}) async-start(bf16[16,256,128]{2,1,0:T(8,128)(2,1)} %get-tuple-element.21), calls=%async_computation | async-start | bytes 2097152 | tf_op jit(solution)/shard_map/all_to_all | solution.py:318
  27.7 0.0 copy-done.3
  27.7 11.6 %key_feats.1.keys = bf16[4096,144]{1,0:T(8,128)(2,1)} custom-call(bf16[96,32,512]{2,1,0:T(8,128)(2,1)} %x_ref.1, bf16[9,96,128]{2,1,0:T(8,128)(2,1)} %bitcast.14, bf16[112,512]{1,0:T(8,128)(2,1)} %copy-done.2, bf16[16,768]{1,0:T(8,128)(2,1)} %copy-done.3), custom_call_target="tpu_custom_call" | custom-call | tf_op jit(solution)/shard_map/key_feats/pallas_call | solution.py:321
  39.3 10.1 %all-to-all-done.query_ref = bf16[16,256,128]{2,1,0:T(8,128)(2,1)S(1)} async-done(((bf16[16,256,128]{2,1,0:T(8,128)(2,1)}), bf16[16,256,128]{2,1,0:T(8,128)(2,1)S(1)}, u32[]{:S(2)}, u32[]{:S(2)}) %all-to-all-start) | async-done | bytes 1048608 | tf_op jit(solution)/shard_map/all_to_all | solution.py:318
  49.4 0.0 copy-start
  49.4 4.1 %collective-permute-start.2 = (bf16[16,256,128]{2,1,0:T(8,128)(2,1)S(1)}, bf16[16,256,128]{2,1,0:T(8,128)(2,1)S(1)}, u32[]{:S(2)}, u32[]{:S(2)}) collective-permute-start(bf16[16,256,128]{2,1,0:T(8,128)(2,1)S(1)} %all-to-all-done.query_ref), channel_id=1, source_target_pairs={{0,8},{8,0},{1,9},{9,1},{2,10},{10,2},{3,11},{11,3},{4,12},{12,4},... | collective-permute-start | bytes 3145736 | tf_op jit(solution)/shard_map/ppermute | solution.py:329
  53.5 0.7 pad_add_fusion.place_ref
  54.1 0.0 copy-done
  54.1 58.5 %attention.2.refs_0_ = f32[16,4,256]{2,1,0:T(4,128)} custom-call(s32[3]{0:T(128)} %pad_add_fusion.place_ref, bf16[16,256,128]{2,1,0:T(8,128)(2,1)} %copy-done, bf16[4096,144]{1,0:T(8,128)(2,1)} %key_feats.1.keys), custom_call_target="tpu_custom_call" | custom-call | tf_op jit(solution)/shard_map/attention/pallas_call | solution.py:351
  112.6 0.0 collective-permute-done.2.query_ref
  112.6 0.0 copy-start.1
  112.6 1.0 copy-done.1
  113.6 58.6 %attention.3 = f32[16,2,4,256]{3,2,1,0:T(4,128)} custom-call(s32[3]{0:T(128)} %pad_add_fusion.place_ref, bf16[16,256,128]{2,1,0:T(8,128)(2,1)} %copy-done.1, bf16[4096,144]{1,0:T(8,128)(2,1)} %key_feats.1.keys, f32[16,4,256]{2,1,0:T(4,128)} %attention.2.refs_0_), custom_call_target="tpu_custom_call" | custom-call | tf_op jit(solution)/shard_map/attention/pallas_call | solution.py:351
  172.2 8.0 %all-to-all-start.1 = ((f32[32,4,256]{2,1,0:T(4,128)}), f32[32,4,256]{2,1,0:T(4,128)S(1)}, u32[]{:S(2)}, u32[]{:S(2)}) async-start(f32[32,4,256]{2,1,0:T(4,128)} %bitcast.15), calls=%async_computation.1 | async-start | bytes 262144 | tf_op jit(solution)/shard_map/all_to_all | solution.py:369
  180.2 10.6 %all-to-all-done.1 = f32[32,4,256]{2,1,0:T(4,128)S(1)} async-done(((f32[32,4,256]{2,1,0:T(4,128)}), f32[32,4,256]{2,1,0:T(4,128)S(1)}, u32[]{:S(2)}, u32[]{:S(2)}) %all-to-all-start.1) | async-done | bytes 131104 | tf_op jit(solution)/shard_map/all_to_all | solution.py:369
  190.8 0.1 slice_reduce_fusion
  190.9 0.1 multiply_exponential_fusion
  190.9 0.1 fusion
  191.0 0.6 broadcast_in_dim.5
  191.6 7.0 %all-to-all-start.2 = ((f32[8,4,256]{2,1,0:T(4,128)}), f32[8,4,256]{2,1,0:T(4,128)S(1)}, u32[]{:S(2)}, u32[]{:S(2)}) async-start(f32[8,4,256]{2,1,0:T(4,128)} %broadcast_in_dim.5), calls=%async_computation.2 | async-start | bytes 65536 | tf_op jit(solution)/shard_map/all_to_all | solution.py:371
  198.6 5.1 %all-to-all-done.2 = f32[8,4,256]{2,1,0:T(4,128)S(1)} async-done(((f32[8,4,256]{2,1,0:T(4,128)}), f32[8,4,256]{2,1,0:T(4,128)S(1)}, u32[]{:S(2)}, u32[]{:S(2)}) %all-to-all-start.2) | async-done | bytes 32800 | tf_op jit(solution)/shard_map/all_to_all | solution.py:371
  203.9 0.1 div.42
  203.9 0.1 div.38
  204.0 0.1 broadcast_subtract_fusion
  204.1 0.6 pad_maximum_fusion.1
  (9 shorter events, 0.1 us)
Async XLA Ops:
  3.3 8.4 %collective-permute-start = (bf16[112,512]{1,0:T(8,128)(2,1)}, bf16[112,512]{1,0:T(8,128)(2,1)S(1)}, u32[]{:S(2)}, u32[]{:S(2)}) collective-permute-start(bf16[112,512]{1,0:T(8,128)(2,1)} %get-tuple-element.17), channel_id=1, source_target_pairs={{0,8},{8,16},{16,24},{24,32},{32,40},{40,48},{48,56},{56,64},{64,7... | collective-permute-start | bytes 344072 | tf_op jit(solution)/shard_map/ppermute | solution.py:309
  11.7 0.6 copy-start.2
  14.4 4.3 %collective-permute-start.1 = (bf16[16,768]{1,0:T(8,128)(2,1)}, bf16[16,768]{1,0:T(8,128)(2,1)S(1)}, u32[]{:S(2)}, u32[]{:S(2)}) collective-permute-start(bf16[16,768]{1,0:T(8,128)(2,1)} %get-tuple-element.20), channel_id=1, source_target_pairs={{0,1},{1,2},{2,3},{3,4},{4,5},{5,6},{6,7},{8,9},{9,10},{10,11},{11... | collective-permute-start | bytes 73736 | tf_op jit(solution)/shard_map/ppermute | solution.py:316
  18.7 9.0 %copy-start.3 = (bf16[16,768]{1,0:T(8,128)(2,1)}, bf16[16,768]{1,0:T(8,128)(2,1)S(1)}, u32[]{:S(2)}) copy-start(bf16[16,768]{1,0:T(8,128)(2,1)S(1)} %collective-permute-done.1.side_ref) | copy-start | bytes 73732
  18.7 30.6 %all-to-all-start = ((bf16[16,256,128]{2,1,0:T(8,128)(2,1)}), bf16[16,256,128]{2,1,0:T(8,128)(2,1)S(1)}, u32[]{:S(2)}, u32[]{:S(2)}) async-start(bf16[16,256,128]{2,1,0:T(8,128)(2,1)} %get-tuple-element.21), calls=%async_computation | async-start | bytes 2097152 | tf_op jit(solution)/shard_map/all_to_all | solution.py:318
  49.4 4.8 %copy-start = (bf16[16,256,128]{2,1,0:T(8,128)(2,1)}, bf16[16,256,128]{2,1,0:T(8,128)(2,1)S(1)}, u32[]{:S(2)}) copy-start(bf16[16,256,128]{2,1,0:T(8,128)(2,1)S(1)} %all-to-all-done.query_ref) | copy-start | bytes 3145732
  49.4 63.3 %collective-permute-start.2 = (bf16[16,256,128]{2,1,0:T(8,128)(2,1)S(1)}, bf16[16,256,128]{2,1,0:T(8,128)(2,1)S(1)}, u32[]{:S(2)}, u32[]{:S(2)}) collective-permute-start(bf16[16,256,128]{2,1,0:T(8,128)(2,1)S(1)} %all-to-all-done.query_ref), channel_id=1, source_target_pairs={{0,8},{8,0},{1,9},{9,1},{2,10},{10,2},{3,11},{11,3},{4,12},{12,4},... | collective-permute-start | bytes 3145736 | tf_op jit(solution)/shard_map/ppermute | solution.py:329
  112.6 1.0 copy-start.1
  172.2 18.6 %all-to-all-start.1 = ((f32[32,4,256]{2,1,0:T(4,128)}), f32[32,4,256]{2,1,0:T(4,128)S(1)}, u32[]{:S(2)}, u32[]{:S(2)}) async-start(f32[32,4,256]{2,1,0:T(4,128)} %bitcast.15), calls=%async_computation.1 | async-start | bytes 262144 | tf_op jit(solution)/shard_map/all_to_all | solution.py:369
  191.6 12.1 %all-to-all-start.2 = ((f32[8,4,256]{2,1,0:T(4,128)}), f32[8,4,256]{2,1,0:T(4,128)S(1)}, u32[]{:S(2)}, u32[]{:S(2)}) async-start(f32[8,4,256]{2,1,0:T(4,128)} %broadcast_in_dim.5), calls=%async_computation.2 | async-start | bytes 65536 | tf_op jit(solution)/shard_map/all_to_all | solution.py:371

commit v5 on v3

--- a/solution.py
+++ b/solution.py
@@ -102,7 +102,7 @@
     side_ref[...] = side.astype(BF16)
 
 
-def spread_kernel(main_ref, edge_ref, down_ref, side_ref, out_ref, corner_ref):
+def join_kernel(main_ref, edge_ref, down_ref, side_ref, out_ref, corner_ref):
     n_query, channels = main_ref.shape
     rows = edge_ref.shape[0] // 2
     half = n_query // rows
@@ -119,9 +119,7 @@
             iota(old.shape, 0) == 0, jnp.broadcast_to(fixed[r : r + 1], old.shape), old
         )
         pieces += [new.astype(BF16), main_ref[r * half + 16 : (r + 1) * half, :]]
-    full = jnp.concatenate(pieces, axis=0)
-    for i in range(out_ref.shape[0]):
-        out_ref[i] = full
+    out_ref[...] = jnp.concatenate(pieces, axis=0)
     row = down_ref[0:channels_in, wide - 128 :]
     row = jnp.concatenate([row, jnp.zeros((depth - channels_in, 128), BF16)], axis=0)
     side = side_ref[...].astype(F32)
@@ -225,11 +223,12 @@
         for p in range(n_block):
             lanes = slice(p * n_query, (p + 1) * n_query)
             block = jnp.concatenate([v[:, lanes] for v in parts], axis=0)
+            there = (place_ref[3] + n_block - p) % n_block
             if second:
-                out_ref[p, 1 - place_ref[2]] = block
+                out_ref[there, 1 - place_ref[2]] = block
                 out_ref[p, place_ref[2]] = other_ref[p]
             else:
-                out_ref[p] = block
+                out_ref[there] = block
 
     sample = jnp.concatenate(
         [keys[i * tile_cols : i * tile_cols + 16, 0:channels] for i in range(tile_rows)], axis=0
@@ -276,8 +275,8 @@
     channels = conv_weight.shape[1]
     tile_rows, tile_cols = rows_in // 2, cols_in // 2
     band_rows, band_cols = (frame_band.shape[1] - 1) // 2, frame_band.shape[2] // 2
-    pb = ("chip", "core")
-    n_chip, n_pb, n_ka = lax.axis_size("chip"), lax.axis_size(pb), lax.axis_size("ka")
+    pb = ("x", "z", "core")
+    n_chip, n_pb, n_ka = lax.axis_size(("x", "z")), lax.axis_size(pb), lax.axis_size("ka")
     row_count, col_count = tile_rows * n_pb, tile_cols * n_ka
     pb_index, ka_index = lax.axis_index(pb), lax.axis_index("ka")
     n_query = band_rows * band_cols
@@ -307,14 +306,21 @@
         name="query_feats",
     )(frame_band.transpose(1, 0, 2), weights, frame_two, frame_two)
     above = lax.ppermute(down, pb, [(i, i + 1) for i in range(n_pb - 1)])
-    copies, right = pl.pallas_call(
-        spread_kernel,
-        out_shape=(jax.ShapeDtypeStruct((n_chip, n_query, channels), BF16), outs[3]),
+    mine, right = pl.pallas_call(
+        join_kernel,
+        out_shape=(outs[0], outs[3]),
         compiler_params=params,
-        name="query_copies",
+        name="query_join",
     )(main, edge, above, right)
     side = lax.ppermute(right, "ka", [(i, i + 1) for i in range(n_ka - 1)])
-    queries = lax.all_to_all(copies, "chip", 0, 0)
+
+    def circled(x, axis):
+        count = lax.axis_size(axis)
+        turns = [[(i, (i + d) % count) for i in range(count)] for d in range(1, count)]
+        return jnp.stack([x] + [lax.ppermute(x, axis, pairs) for pairs in turns])
+
+    near, side = lax.optimization_barrier((circled(mine, "z"), side))
+    queries = circled(near, "x").reshape(n_chip, n_query, channels)
 
     n_key = tile_rows * tile_cols
     keys = pl.pallas_call(
@@ -328,38 +334,56 @@
     twins = lax.ppermute(queries, "core", [(0, 1), (1, 0)])
 
     place = jnp.stack(
-        [pb_index * tile_rows, ka_index * tile_cols, lax.axis_index("core")]
+        [
+            pb_index * tile_rows,
+            ka_index * tile_cols,
+            lax.axis_index("core"),
+            lax.axis_index("z"),
+            lax.axis_index("x"),
+        ]
     ).astype(jnp.int32)
-    n_block = 4
+    n_block, n_x = lax.axis_size("z"), lax.axis_size("x")
     scale = math.log2(math.e) / math.sqrt(channels)
 
     def attend(block, other):
+        def there(i, place):
+            return (place[4] + n_x - i) % n_x
+
         ins = [keys]
         in_specs = [
-            pl.BlockSpec(memory_space=pltpu.SMEM),
-            pl.BlockSpec((n_block, n_query, channels), lambda i: (i, 0, 0)),
-        ] + [whole(v.shape) for v in ins]
+            pl.BlockSpec((n_block, n_query, channels), lambda i, place: (i, 0, 0)),
+            whole(keys.shape),
+        ]
         if other is None:
-            out_spec = pl.BlockSpec((n_block, 4, n_query), lambda i: (i, 0, 0))
+            out_spec = pl.BlockSpec(
+                (n_block, 4, n_query), lambda i, place: (there(i, place), 0, 0)
+            )
             out_shape = (n_chip, 4, n_query)
         else:
             ins.append(other)
-            in_specs.append(pl.BlockSpec((n_block, 4, n_query), lambda i: (i, 0, 0)))
-            out_spec = pl.BlockSpec((n_block, 2, 4, n_query), lambda i: (i, 0, 0, 0))
+            in_specs.append(
+                pl.BlockSpec((n_block, 4, n_query), lambda i, place: (there(i, place), 0, 0))
+            )
+            out_spec = pl.BlockSpec(
+                (n_block, 2, 4, n_query), lambda i, place: (there(i, place), 0, 0, 0)
+            )
             out_shape = (n_chip, 2, 4, n_query)
         return pl.pallas_call(
             functools.partial(
                 attention_kernel,
                 tile_rows, float(row_count), float(col_count), scale, other is not None,
             ),
-            grid=(n_chip // n_block,),
-            in_specs=in_specs,
-            out_specs=out_spec,
+            grid_spec=pltpu.PrefetchScalarGridSpec(
+                num_scalar_prefetch=1,
+                grid=(n_x,),
+                in_specs=in_specs,
+                out_specs=out_spec,
+                scratch_shapes=[
+                    pltpu.VMEM((channels + 16, n_block * n_query), BF16),
+                    pltpu.VMEM((2 + int(math.log2(tile_cols // 8)), 8, n_block * n_query), F32),
+                ],
+            ),
             out_shape=jax.ShapeDtypeStruct(out_shape, F32),
-            scratch_shapes=[
-                pltpu.VMEM((channels + 16, n_block * n_query), BF16),
-                pltpu.VMEM((2 + int(math.log2(tile_cols // 8)), 8, n_block * n_query), F32),
-            ],
             compiler_params=params,
             name="attention",
         )(place, block, *ins)
@@ -383,9 +407,9 @@
 def solution(mesh):
     n_pb, n_ka = mesh.shape["pb"], mesh.shape["ka"]
     finer = jax.sharding.Mesh(
-        mesh.devices.reshape(n_pb // 2, 2, n_ka), ("chip", "core", "ka")
-    )
-    pb = ("chip", "core")
+        mesh.devices.reshape(n_pb // 8, 4, 2, n_ka), ("x", "z", "core", "ka")
+    )
+    pb = ("x", "z", "core")
     in_specs = (P(None, pb, "ka"), P(None, None, pb), P())
     out_specs = P(None, None, pb)
     return jax.shard_map(

time: 212 us -> 199 us (0.939)
  starting transfers between devices: 47.8 us -> 34.1 us
    all_to_all x1, starting transfers between devices: 18.7 us -> 4.97 us  [on_device(): final = merged(lax.all_to_all(copies, 'ka', 0, 0), scale)]
    ppermute x0 -> x6, starting transfers between devices: none -> 11.6 us  [circled(): return jnp.stack([x] + [lax.ppermute(x, axis, pairs) for pairs in turns])]
    all_to_all x1 -> x0, starting transfers between devices: 8.94 us -> none  [on_device(): queries = lax.all_to_all(copies, 'chip', 0, 0)]
    all_to_all x1 -> x0, waiting for transfers between devices: 6.08 us -> none  [on_device(): queries = lax.all_to_all(copies, 'chip', 0, 0)]
    ppermute x0 -> x6, waiting for transfers between devices: none -> 5.49 us  [circled(): return jnp.stack([x] + [lax.ppermute(x, axis, pairs) for pairs in turns])]
  transfers between devices with their start and end apart: 6 -> 11, of which waited for: 5 -> 5; matrix products, arithmetic and copies ran while one was open for 0% -> 1% of each run, Pallas kernels for 33% -> 36%
where the time goes in v5:
time: 199 us; the launch traced here: 198 us
  Pallas kernels  135 us (68%)
  starting transfers between devices  34.1 us (17%)
  waiting for transfers between devices  24.1 us (12%)
  local copies, waits for them, and re-layouts  3.03 us (2%)
    pallas_call x2, Pallas kernels, attend(): pl.pallas_call(functools.partial(attention_kernel, tile_rows, float(row_c...  118 us
    ppermute x6, starting transfers between devices, circled(): return jnp.stack([x] + [lax.ppermute(x, axis, pairs) for pairs in turns])  11.6 us
    pallas_call x1, Pallas kernels, on_device(): pl.pallas_call(key_kernel, out_shape=jax.ShapeDtypeStruct((n_key, channel...  11.6 us
    all_to_all x1, waiting for transfers between devices, on_device(): mine = merged(lax.all_to_all(states, pb, 0, 0), scale)  11.3 us
    all_to_all x1, starting transfers between devices, on_device(): mine = merged(lax.all_to_all(states, pb, 0, 0), scale)  6.78 us
    ppermute x1, starting transfers between devices, on_device(): above = lax.ppermute(down, pb, [(i, i + 1) for i in range(n_pb - 1)])  6.29 us
    ppermute x6, waiting for transfers between devices, circled(): return jnp.stack([x] + [lax.ppermute(x, axis, pairs) for pairs in turns])  5.49 us
    all_to_all x1, waiting for transfers between devices, on_device(): final = merged(lax.all_to_all(copies, 'ka', 0, 0), scale)  5.16 us
  transfers between devices with their start and end apart: 11, of which 5 were waited for; matrix products, arithmetic and copies ran while one was open for 1% of the time, Pallas kernels for 36%

profile of v5, /device:TPU:1, one launch (start us, length us, event | category | flops | bytes accessed | tf_op | source)
XLA Modules:
  0.0 198.3 jit_solution(16455581580102449502)
XLA Ops:
  0.0 3.3 %query_feats.1 = (bf16[256,128]{1,0:T(8,128)(2,1)}, f32[8,128]{1,0:T(8,128)}, bf16[112,512]{1,0:T(8,128)(2,1)}, bf16[16,768]{1,0:T(8,128)(2,1)}) custom-call(bf16[9,96,128]{2,1,0:T(8,128)(2,1)} %bitcast.33, bf16[9,96,128]{2,1,0:T(8,128)(2,1)} %bitcast.27, bf16[96,32,512]{2,1,0:T(8,128)(2,1)} %x_ref.1, bf16[96,32,512]{2,1,0:T(8,128)(2,1)} %x_ref.1), custom_call_target="tpu_custom_call" | custom-call | tf_op jit(solution)/shard_map/query_feats/pallas_call | solution.py:294
  3.3 6.3 %collective-permute-start = (bf16[112,512]{1,0:T(8,128)(2,1)}, bf16[112,512]{1,0:T(8,128)(2,1)S(1)}, u32[]{:S(2)}, u32[]{:S(2)}) collective-permute-start(bf16[112,512]{1,0:T(8,128)(2,1)} %get-tuple-element.17), channel_id=1, source_target_pairs={{0,8},{8,16},{16,24},{24,32},{32,40},{40,48},{48,56},{56,64},{64,7... | collective-permute-start | bytes 344072 | tf_op jit(solution)/shard_map/ppermute | solution.py:308
  9.6 2.1 %collective-permute-done.down_ref.above_ref = bf16[112,512]{1,0:T(8,128)(2,1)S(1)} collective-permute-done((bf16[112,512]{1,0:T(8,128)(2,1)}, bf16[112,512]{1,0:T(8,128)(2,1)S(1)}, u32[]{:S(2)}, u32[]{:S(2)}) %collective-permute-start) | collective-permute-done | bytes 114720 | tf_op jit(solution)/shard_map/ppermute | solution.py:308
  11.7 0.0 copy-start.2
  11.7 0.6 copy-done.2
  12.3 1.7 query_join.1
  14.0 2.5 %collective-permute-start.3 = (bf16[256,128]{1,0:T(8,128)(2,1)}, bf16[256,128]{1,0:T(8,128)(2,1)S(1)}, u32[]{:S(2)}, u32[]{:S(2)}) collective-permute-start(bf16[256,128]{1,0:T(8,128)(2,1)} %get-tuple-element.19), channel_id=1, source_target_pairs={{0,48},{16,0},{32,16},{48,32},{1,49},{17,1},{33,17},{49,33},{2,50}... | collective-permute-start | bytes 196616 | tf_op jit(solution)/shard_map/ppermute | solution.py:320
  16.5 5.3 %collective-permute-start.2 = (bf16[256,128]{1,0:T(8,128)(2,1)}, bf16[256,128]{1,0:T(8,128)(2,1)S(1)}, u32[]{:S(2)}, u32[]{:S(2)}) collective-permute-start(bf16[256,128]{1,0:T(8,128)(2,1)} %get-tuple-element.19), channel_id=1, source_target_pairs={{0,32},{16,48},{32,0},{48,16},{1,33},{17,49},{33,1},{49,17},{2,34}... | collective-permute-start | bytes 196616 | tf_op jit(solution)/shard_map/ppermute | solution.py:320
  21.8 0.0 collective-permute-start.1
  21.8 3.2 %collective-permute-start.4 = (bf16[16,768]{1,0:T(8,128)(2,1)}, bf16[16,768]{1,0:T(8,128)(2,1)S(1)}, u32[]{:S(2)}, u32[]{:S(2)}) collective-permute-start(bf16[16,768]{1,0:T(8,128)(2,1)} %get-tuple-element.20), channel_id=1, source_target_pairs={{0,1},{1,2},{2,3},{3,4},{4,5},{5,6},{6,7},{8,9},{9,10},{10,11},{11... | collective-permute-start | bytes 73736 | tf_op jit(solution)/shard_map/ppermute | solution.py:315
  25.0 0.0 collective-permute-done.3
  25.0 0.0 collective-permute-done.2
  25.0 3.1 %collective-permute-done.1 = bf16[256,128]{1,0:T(8,128)(2,1)S(1)} collective-permute-done((bf16[256,128]{1,0:T(8,128)(2,1)}, bf16[256,128]{1,0:T(8,128)(2,1)S(1)}, u32[]{:S(2)}, u32[]{:S(2)}) %collective-permute-start.1) | collective-permute-done | bytes 65568 | tf_op jit(solution)/shard_map/ppermute | solution.py:320
  28.2 0.9 pad_maximum_fusion.1
  29.0 0.0 collective-permute-done.4.side_ref
  29.1 0.0 copy-start.3
  29.1 3.1 %collective-permute-start.7 = (bf16[4,256,128]{2,1,0:T(8,128)(2,1)S(1)}, bf16[4,256,128]{2,1,0:T(8,128)(2,1)S(1)}, u32[]{:S(2)}, u32[]{:S(2)}) collective-permute-start(bf16[4,256,128]{2,1,0:T(8,128)(2,1)S(1)} %pad_maximum_fusion.1), channel_id=1, source_target_pairs={{0,192},{64,0},{128,64},{192,128},{1,193},{65,1},{129,65},{193,129... | collective-permute-start | bytes 786440 | tf_op jit(solution)/shard_map/ppermute | solution.py:320
  32.2 0.0 collective-permute-start.6
  32.2 0.7 collective-permute-start.5
  32.9 0.0 copy-done.3
  32.9 11.6 %key_feats.1.keys = bf16[4096,144]{1,0:T(8,128)(2,1)} custom-call(bf16[96,32,512]{2,1,0:T(8,128)(2,1)} %x_ref.1, bf16[9,96,128]{2,1,0:T(8,128)(2,1)} %bitcast.28, bf16[112,512]{1,0:T(8,128)(2,1)} %copy-done.2, bf16[16,768]{1,0:T(8,128)(2,1)} %copy-done.3), custom_call_target="tpu_custom_call" | custom-call | tf_op jit(solution)/shard_map/key_feats/pallas_call | solution.py:326
  44.4 0.0 collective-permute-done.7
  44.5 0.0 collective-permute-done.6
  44.5 2.4 %collective-permute-done.5 = bf16[4,256,128]{2,1,0:T(8,128)(2,1)S(1)} collective-permute-done((bf16[4,256,128]{2,1,0:T(8,128)(2,1)S(1)}, bf16[4,256,128]{2,1,0:T(8,128)(2,1)S(1)}, u32[]{:S(2)}, u32[]{:S(2)}) %collective-permute-start.5) | collective-permute-done | bytes 262176 | tf_op jit(solution)/shard_map/ppermute | solution.py:320
  46.8 0.1 pad_maximum_fusion
  47.0 0.0 copy-start
  47.0 1.2 collective-permute-start.8
  48.2 0.6 stack.58.place_ref
  48.8 0.0 copy-done
  48.8 59.2 %attention.2.refs_0_ = f32[16,4,256]{2,1,0:T(4,128)} custom-call(s32[5]{0:T(128)} %stack.58.place_ref, bf16[16,256,128]{2,1,0:T(8,128)(2,1)} %bitcast.25, bf16[4096,144]{1,0:T(8,128)(2,1)} %key_feats.1.keys), custom_call_target="tpu_custom_call" | custom-call | tf_op jit(solution)/shard_map/attention/pallas_call | solution.py:371
  108.0 0.0 collective-permute-done.8.query_ref
  108.0 0.0 copy-start.1
  108.0 1.0 copy-done.1
  109.0 59.3 %attention.3 = f32[16,2,4,256]{3,2,1,0:T(4,128)} custom-call(s32[5]{0:T(128)} %stack.58.place_ref, bf16[16,256,128]{2,1,0:T(8,128)(2,1)} %copy-done.1, bf16[4096,144]{1,0:T(8,128)(2,1)} %key_feats.1.keys, f32[16,4,256]{2,1,0:T(4,128)} %attention.2.refs_0_), custom_call_target="tpu_custom_call" | custom-call | tf_op jit(solution)/shard_map/attention/pallas_call | solution.py:371
  168.3 6.8 %all-to-all-start = ((f32[32,4,256]{2,1,0:T(4,128)}), f32[32,4,256]{2,1,0:T(4,128)S(1)}, u32[]{:S(2)}, u32[]{:S(2)}) async-start(f32[32,4,256]{2,1,0:T(4,128)} %bitcast.29), calls=%async_computation | async-start | bytes 262144 | tf_op jit(solution)/shard_map/all_to_all | solution.py:392
  175.1 11.3 %all-to-all-done = f32[32,4,256]{2,1,0:T(4,128)S(1)} async-done(((f32[32,4,256]{2,1,0:T(4,128)}), f32[32,4,256]{2,1,0:T(4,128)S(1)}, u32[]{:S(2)}, u32[]{:S(2)}) %all-to-all-start) | async-done | bytes 131104 | tf_op jit(solution)/shard_map/all_to_all | solution.py:392
  186.4 0.1 slice_reduce_fusion
  186.5 0.1 multiply_exponential_fusion
  186.6 0.1 fusion
  186.6 0.6 broadcast_in_dim.5
  187.3 5.0 %all-to-all-start.1 = ((f32[8,4,256]{2,1,0:T(4,128)}), f32[8,4,256]{2,1,0:T(4,128)S(1)}, u32[]{:S(2)}, u32[]{:S(2)}) async-start(f32[8,4,256]{2,1,0:T(4,128)} %broadcast_in_dim.5), calls=%async_computation.1 | async-start | bytes 65536 | tf_op jit(solution)/shard_map/all_to_all | solution.py:394
  192.2 5.2 %all-to-all-done.1 = f32[8,4,256]{2,1,0:T(4,128)S(1)} async-done(((f32[8,4,256]{2,1,0:T(4,128)}), f32[8,4,256]{2,1,0:T(4,128)S(1)}, u32[]{:S(2)}, u32[]{:S(2)}) %all-to-all-start.1) | async-done | bytes 32800 | tf_op jit(solution)/shard_map/all_to_all | solution.py:394
  197.5 0.1 div.42
  197.6 0.1 div.38
  197.7 0.1 broadcast_subtract_fusion
  197.7 0.6 pad_maximum_fusion.3
  (9 shorter events, 0.1 us)
Async XLA Ops:
  3.3 8.4 %collective-permute-start = (bf16[112,512]{1,0:T(8,128)(2,1)}, bf16[112,512]{1,0:T(8,128)(2,1)S(1)}, u32[]{:S(2)}, u32[]{:S(2)}) collective-permute-start(bf16[112,512]{1,0:T(8,128)(2,1)} %get-tuple-element.17), channel_id=1, source_target_pairs={{0,8},{8,16},{16,24},{24,32},{32,40},{40,48},{48,56},{56,64},{64,7... | collective-permute-start | bytes 344072 | tf_op jit(solution)/shard_map/ppermute | solution.py:308
  11.7 0.6 copy-start.2
  14.0 11.0 %collective-permute-start.3 = (bf16[256,128]{1,0:T(8,128)(2,1)}, bf16[256,128]{1,0:T(8,128)(2,1)S(1)}, u32[]{:S(2)}, u32[]{:S(2)}) collective-permute-start(bf16[256,128]{1,0:T(8,128)(2,1)} %get-tuple-element.19), channel_id=1, source_target_pairs={{0,48},{16,0},{32,16},{48,32},{1,49},{17,1},{33,17},{49,33},{2,50}... | collective-permute-start | bytes 196616 | tf_op jit(solution)/shard_map/ppermute | solution.py:320
  16.5 8.6 %collective-permute-start.2 = (bf16[256,128]{1,0:T(8,128)(2,1)}, bf16[256,128]{1,0:T(8,128)(2,1)S(1)}, u32[]{:S(2)}, u32[]{:S(2)}) collective-permute-start(bf16[256,128]{1,0:T(8,128)(2,1)} %get-tuple-element.19), channel_id=1, source_target_pairs={{0,32},{16,48},{32,0},{48,16},{1,33},{17,49},{33,1},{49,17},{2,34}... | collective-permute-start | bytes 196616 | tf_op jit(solution)/shard_map/ppermute | solution.py:320
  21.8 6.3 %collective-permute-start.1 = (bf16[256,128]{1,0:T(8,128)(2,1)}, bf16[256,128]{1,0:T(8,128)(2,1)S(1)}, u32[]{:S(2)}, u32[]{:S(2)}) collective-permute-start(bf16[256,128]{1,0:T(8,128)(2,1)} %get-tuple-element.19), channel_id=1, source_target_pairs={{0,16},{16,32},{32,48},{48,0},{1,17},{17,33},{33,49},{49,1},{2,18}... | collective-permute-start | bytes 196616 | tf_op jit(solution)/shard_map/ppermute | solution.py:320
  21.8 7.2 %collective-permute-start.4 = (bf16[16,768]{1,0:T(8,128)(2,1)}, bf16[16,768]{1,0:T(8,128)(2,1)S(1)}, u32[]{:S(2)}, u32[]{:S(2)}) collective-permute-start(bf16[16,768]{1,0:T(8,128)(2,1)} %get-tuple-element.20), channel_id=1, source_target_pairs={{0,1},{1,2},{2,3},{3,4},{4,5},{5,6},{6,7},{8,9},{9,10},{10,11},{11... | collective-permute-start | bytes 73736 | tf_op jit(solution)/shard_map/ppermute | solution.py:315
  29.1 3.8 %copy-start.3 = (bf16[16,768]{1,0:T(8,128)(2,1)}, bf16[16,768]{1,0:T(8,128)(2,1)S(1)}, u32[]{:S(2)}) copy-start(bf16[16,768]{1,0:T(8,128)(2,1)S(1)} %collective-permute-done.4.side_ref) | copy-start | bytes 73732
  29.1 15.4 %collective-permute-start.7 = (bf16[4,256,128]{2,1,0:T(8,128)(2,1)S(1)}, bf16[4,256,128]{2,1,0:T(8,128)(2,1)S(1)}, u32[]{:S(2)}, u32[]{:S(2)}) collective-permute-start(bf16[4,256,128]{2,1,0:T(8,128)(2,1)S(1)} %pad_maximum_fusion.1), channel_id=1, source_target_pairs={{0,192},{64,0},{128,64},{192,128},{1,193},{65,1},{129,65},{193,129... | collective-permute-start | bytes 786440 | tf_op jit(solution)/shard_map/ppermute | solution.py:320
  32.2 12.3 %collective-permute-start.6 = (bf16[4,256,128]{2,1,0:T(8,128)(2,1)S(1)}, bf16[4,256,128]{2,1,0:T(8,128)(2,1)S(1)}, u32[]{:S(2)}, u32[]{:S(2)}) collective-permute-start(bf16[4,256,128]{2,1,0:T(8,128)(2,1)S(1)} %pad_maximum_fusion.1), channel_id=1, source_target_pairs={{0,128},{64,192},{128,0},{192,64},{1,129},{65,193},{129,1},{193,65... | collective-permute-start | bytes 786440 | tf_op jit(solution)/shard_map/ppermute | solution.py:320
  32.2 14.6 %collective-permute-start.5 = (bf16[4,256,128]{2,1,0:T(8,128)(2,1)S(1)}, bf16[4,256,128]{2,1,0:T(8,128)(2,1)S(1)}, u32[]{:S(2)}, u32[]{:S(2)}) collective-permute-start(bf16[4,256,128]{2,1,0:T(8,128)(2,1)S(1)} %pad_maximum_fusion.1), channel_id=1, source_target_pairs={{0,64},{64,128},{128,192},{192,0},{1,65},{65,129},{129,193},{193,1... | collective-permute-start | bytes 786440 | tf_op jit(solution)/shard_map/ppermute | solution.py:320
  47.0 1.8 copy-start
  47.0 61.1 %collective-permute-start.8 = (bf16[16,256,128]{2,1,0:T(8,128)(2,1)S(1)}, bf16[16,256,128]{2,1,0:T(8,128)(2,1)S(1)}, u32[]{:S(2)}, u32[]{:S(2)}) collective-permute-start(bf16[16,256,128]{2,1,0:T(8,128)(2,1)S(1)} %bitcast.24), channel_id=1, source_target_pairs={{0,8},{8,0},{1,9},{9,1},{2,10},{10,2},{3,11},{11,3},{4,12},{12,4},... | collective-permute-start | bytes 3145736 | tf_op jit(solution)/shard_map/ppermute | solution.py:334
  108.0 1.0 copy-start.1
  168.3 18.1 %all-to-all-start = ((f32[32,4,256]{2,1,0:T(4,128)}), f32[32,4,256]{2,1,0:T(4,128)S(1)}, u32[]{:S(2)}, u32[]{:S(2)}) async-start(f32[32,4,256]{2,1,0:T(4,128)} %bitcast.29), calls=%async_computation | async-start | bytes 262144 | tf_op jit(solution)/shard_map/all_to_all | solution.py:392
  187.3 10.1 %all-to-all-start.1 = ((f32[8,4,256]{2,1,0:T(4,128)}), f32[8,4,256]{2,1,0:T(4,128)S(1)}, u32[]{:S(2)}, u32[]{:S(2)}) async-start(f32[8,4,256]{2,1,0:T(4,128)} %broadcast_in_dim.5), calls=%async_computation.1 | async-start | bytes 65536 | tf_op jit(solution)/shard_map/all_to_all | solution.py:394

commit v6 on v5

--- a/solution.py
+++ b/solution.py
@@ -126,30 +126,40 @@
     corner_ref[...] = jnp.where(iota(side.shape, 0) == 8, last_lane(row), side).astype(BF16)
 
 
-def key_kernel(x_ref, w_ref, above_ref, side_ref, key_ref, band_ref):
-    channels_in, rows_in, cols = x_ref.shape
-    half = cols // 2
-    channels = w_ref.shape[2]
-    depth = channels_in * GROUP
-    outs = GROUP // 2
-    n_group = rows_in // GROUP
+def weight_kernel(w_ref, band_ref):
+    _, depth, wide = band_ref.shape
+    _, channels_in, channels = w_ref.shape
     expand = (iota((depth, channels_in), 0) // GROUP == iota((depth, channels_in), 1)).astype(BF16)
     row = iota((depth, channels), 0) % GROUP
     for b in range(3):
         spread = [dot(expand, w_ref[3 * a + b]) for a in range(3)]
-        for i in range(outs + 1):
+        for i in range(wide // channels):
             block = jnp.zeros((depth, channels), F32)
             for a in range(3):
                 block = jnp.where(row == 2 * i - 1 + a, spread[a], block)
             band_ref[b, :, i * channels : (i + 1) * channels] = block.astype(BF16)
-    selector = tap_selector(cols)
+
+
+def key_kernel(x_ref, w_ref, band_ref, above_ref, side_ref, key_ref):
+    channels_in, rows_in, cols = x_ref.shape
+    half = cols // 2
+    channels = w_ref.shape[2]
+    outs = GROUP // 2
+    n_group = rows_in // GROUP
+    block = min(cols, 256)
+    place = iota((block, block), 0)
+    parity = place // (block // 2)
+    source = 2 * (place - parity * (block // 2)) + parity
+    selector = (iota((block, block), 1) == source).astype(BF16)
     side = side_ref[...].astype(F32)
 
     def taps(x, left):
-        picked = dot_nt(selector, x)
-        first = picked[0:half]
+        picked = [dot_nt(selector, x[:, c : c + block]) for c in range(0, cols, block)]
+        even = jnp.concatenate([v[0 : block // 2] for v in picked], axis=0)
+        odd = jnp.concatenate([v[block // 2 :] for v in picked], axis=0)
+        first = pltpu.roll(odd, 1, 0)
         first = jnp.where(iota(first.shape, 0) == 0, jnp.broadcast_to(left, first.shape), first)
-        return first.astype(BF16), picked[half : 2 * half].astype(BF16), picked[2 * half :].astype(BF16)
+        return first.astype(BF16), even.astype(BF16), odd.astype(BF16)
 
     upper = taps(above_ref[0:channels_in, :], side[8:9, 0:channels_in])
     carried = sum(dot(upper[b], w_ref[b]) for b in range(3))
@@ -306,6 +316,14 @@
         name="query_feats",
     )(frame_band.transpose(1, 0, 2), weights, frame_two, frame_two)
     above = lax.ppermute(down, pb, [(i, i + 1) for i in range(n_pb - 1)])
+    later, edge = lax.optimization_barrier((weights, edge))
+    bands = pl.pallas_call(
+        weight_kernel,
+        out_shape=jax.ShapeDtypeStruct((3, depth, (GROUP // 2 + 1) * channels), BF16),
+        compiler_params=params,
+        name="key_weights",
+    )(later)
+    main, bands = lax.optimization_barrier((main, bands))
     mine, right = pl.pallas_call(
         join_kernel,
         out_shape=(outs[0], outs[3]),
@@ -326,10 +344,9 @@
     keys = pl.pallas_call(
         key_kernel,
         out_shape=jax.ShapeDtypeStruct((n_key, channels + 16), BF16),
-        scratch_shapes=[pltpu.VMEM((3, depth, (GROUP // 2 + 1) * channels), BF16)],
         compiler_params=params,
         name="key_feats",
-    )(frame_two, weights, above, side)
+    )(frame_two, weights, bands, above, side)
     queries, keys = lax.optimization_barrier((queries, keys))
     twins = lax.ppermute(queries, "core", [(0, 1), (1, 0)])
 

time: 199 us -> 197 us (0.990)
  waiting for transfers between devices: 24.1 us -> 17.4 us
  starting transfers between devices: 34.1 us -> 37.3 us
    ppermute x6, waiting for transfers between devices: 5.49 us -> 0.91 us  [circled(): return jnp.stack([x] + [lax.ppermute(x, axis, pairs) for pairs in turns])]
    pallas_call x0 -> x1, Pallas kernels: none -> 3.86 us  [on_device(): pl.pallas_call(weight_kernel, out_shape=jax.ShapeDtypeStruct((3, depth, (...]
    ppermute x1, starting transfers between devices: 1.23 us -> 4.16 us  [on_device(): twins = lax.ppermute(queries, 'core', [(0, 1), (1, 0)])]
    pallas_call x1, Pallas kernels: 11.6 us -> 9.05 us  [on_device(): pl.pallas_call(key_kernel, out_shape=jax.ShapeDtypeStruct((n_key, channel...]
    ppermute x1, waiting for transfers between devices: 2.09 us -> 0.01 us  [on_device(): above = lax.ppermute(down, pb, [(i, i + 1) for i in range(n_pb - 1)])]
  transfers between devices with their start and end apart: 11 -> 11, of which waited for: 5 -> 3; matrix products, arithmetic and copies ran while one was open for 1% -> 1% of each run, Pallas kernels for 36% -> 37%
where the time goes in v6:
time: 197 us; the launch traced here: 196 us
  Pallas kernels  136 us (69%)
  starting transfers between devices  37.3 us (19%)
  waiting for transfers between devices  17.4 us (9%)
  local copies, waits for them, and re-layouts  3.03 us (2%)
  other arithmetic  1.98 us (1%)
    pallas_call x2, Pallas kernels, attend(): pl.pallas_call(functools.partial(attention_kernel, tile_rows, float(row_c...  119 us
    ppermute x6, starting transfers between devices, circled(): return jnp.stack([x] + [lax.ppermute(x, axis, pairs) for pairs in turns])  12.4 us
    all_to_all x1, waiting for transfers between devices, on_device(): mine = merged(lax.all_to_all(states, pb, 0, 0), scale)  11.3 us
    pallas_call x1, Pallas kernels, on_device(): pl.pallas_call(key_kernel, out_shape=jax.ShapeDtypeStruct((n_key, channel...  9.05 us
    all_to_all x1, starting transfers between devices, on_device(): mine = merged(lax.all_to_all(states, pb, 0, 0), scale)  7.66 us
    ppermute x1, starting transfers between devices, on_device(): above = lax.ppermute(down, pb, [(i, i + 1) for i in range(n_pb - 1)])  6.29 us
    all_to_all x1, waiting for transfers between devices, on_device(): final = merged(lax.all_to_all(copies, 'ka', 0, 0), scale)  5.1 us
    ppermute x1, starting transfers between devices, on_device(): twins = lax.ppermute(queries, 'core', [(0, 1), (1, 0)])  4.16 us
  transfers between devices with their start and end apart: 11, of which 3 were waited for; matrix products, arithmetic and copies ran while one was open for 1% of the time, Pallas kernels for 37%

profile of v6, /device:TPU:1, one launch (start us, length us, event | category | flops | bytes accessed | tf_op | source)
XLA Modules:
  0.0 196.1 jit_solution(17552156213537895986)
XLA Ops:
  0.0 3.3 %query_feats.1 = (bf16[256,128]{1,0:T(8,128)(2,1)}, f32[8,128]{1,0:T(8,128)}, bf16[112,512]{1,0:T(8,128)(2,1)}, bf16[16,768]{1,0:T(8,128)(2,1)}) custom-call(bf16[9,96,128]{2,1,0:T(8,128)(2,1)} %bitcast.34, bf16[9,96,128]{2,1,0:T(8,128)(2,1)} %bitcast.26, bf16[96,32,512]{2,1,0:T(8,128)(2,1)} %x_ref.1, bf16[96,32,512]{2,1,0:T(8,128)(2,1)} %x_ref.1), custom_call_target="tpu_custom_call" | custom-call | tf_op jit(solution)/shard_map/query_feats/pallas_call | solution.py:304
  3.3 6.3 %collective-permute-start = (bf16[112,512]{1,0:T(8,128)(2,1)}, bf16[112,512]{1,0:T(8,128)(2,1)S(1)}, u32[]{:S(2)}, u32[]{:S(2)}) collective-permute-start(bf16[112,512]{1,0:T(8,128)(2,1)} %get-tuple-element.24), channel_id=1, source_target_pairs={{0,8},{8,16},{16,24},{24,32},{32,40},{40,48},{48,56},{56,64},{64,7... | collective-permute-start | bytes 344072 | tf_op jit(solution)/shard_map/ppermute | solution.py:318
  9.6 3.9 %key_weights.1.band_ref = bf16[3,768,640]{2,1,0:T(8,128)(2,1)} custom-call(bf16[9,96,128]{2,1,0:T(8,128)(2,1)} %bitcast.27), custom_call_target="tpu_custom_call" | custom-call | tf_op jit(solution)/shard_map/key_weights/pallas_call | solution.py:320
  13.4 0.0 collective-permute-done.down_ref.above_ref
  13.4 0.0 copy-start.2
  13.4 0.6 copy-done.2
  14.1 1.7 query_join.1
  15.8 2.5 %collective-permute-start.3 = (bf16[256,128]{1,0:T(8,128)(2,1)}, bf16[256,128]{1,0:T(8,128)(2,1)S(1)}, u32[]{:S(2)}, u32[]{:S(2)}) collective-permute-start(bf16[256,128]{1,0:T(8,128)(2,1)} %get-tuple-element.26), channel_id=1, source_target_pairs={{0,48},{16,0},{32,16},{48,32},{1,49},{17,1},{33,17},{49,33},{2,50}... | collective-permute-start | bytes 196616 | tf_op jit(solution)/shard_map/ppermute | solution.py:338
  18.3 1.7 collective-permute-start.1
  20.0 3.3 %collective-permute-start.2 = (bf16[256,128]{1,0:T(8,128)(2,1)}, bf16[256,128]{1,0:T(8,128)(2,1)S(1)}, u32[]{:S(2)}, u32[]{:S(2)}) collective-permute-start(bf16[256,128]{1,0:T(8,128)(2,1)} %get-tuple-element.26), channel_id=1, source_target_pairs={{0,32},{16,48},{32,0},{48,16},{1,33},{17,49},{33,1},{49,17},{2,34}... | collective-permute-start | bytes 196616 | tf_op jit(solution)/shard_map/ppermute | solution.py:338
  23.3 3.2 %collective-permute-start.4 = (bf16[16,768]{1,0:T(8,128)(2,1)}, bf16[16,768]{1,0:T(8,128)(2,1)S(1)}, u32[]{:S(2)}, u32[]{:S(2)}) collective-permute-start(bf16[16,768]{1,0:T(8,128)(2,1)} %get-tuple-element.27), channel_id=1, source_target_pairs={{0,1},{1,2},{2,3},{3,4},{4,5},{5,6},{6,7},{8,9},{9,10},{10,11},{11... | collective-permute-start | bytes 73736 | tf_op jit(solution)/shard_map/ppermute | solution.py:333
  26.5 0.0 collective-permute-done.3
  26.5 0.0 collective-permute-done.1
  26.5 0.9 collective-permute-done.2
  27.4 0.9 pad_maximum_fusion.1
  28.3 0.0 collective-permute-done.4.side_ref
  28.3 0.0 copy-start.3
  28.3 1.3 collective-permute-start.5
  29.6 2.4 %collective-permute-start.6 = (bf16[4,256,128]{2,1,0:T(8,128)(2,1)S(1)}, bf16[4,256,128]{2,1,0:T(8,128)(2,1)S(1)}, u32[]{:S(2)}, u32[]{:S(2)}) collective-permute-start(bf16[4,256,128]{2,1,0:T(8,128)(2,1)S(1)} %pad_maximum_fusion.1), channel_id=1, source_target_pairs={{0,128},{64,192},{128,0},{192,64},{1,129},{65,193},{129,1},{193,65... | collective-permute-start | bytes 786440 | tf_op jit(solution)/shard_map/ppermute | solution.py:338
  32.0 1.2 collective-permute-start.7
  33.2 0.0 copy-done.3
  33.2 9.1 %key_feats.1.keys = bf16[4096,144]{1,0:T(8,128)(2,1)} custom-call(bf16[96,32,512]{2,1,0:T(8,128)(2,1)} %x_ref.1, bf16[9,96,128]{2,1,0:T(8,128)(2,1)} %bitcast.28, bf16[3,768,640]{2,1,0:T(8,128)(2,1)} %key_weights.1.band_ref, bf16[112,512]{1,0:T(8,128)(2,1)} %copy-done.2, bf16[16,768]{1,0:T(8,128)(2,1)} %copy-done.3), custom_call_target="tpu_custom_call" | custom-call | tf_op jit(solution)/shard_map/key_feats/pallas_call | solution.py:344
  42.3 0.0 collective-permute-done.5
  42.3 0.0 collective-permute-done.6
  42.3 0.0 collective-permute-done.7
  42.3 0.1 pad_maximum_fusion
  42.4 0.0 copy-start
  42.4 4.2 %collective-permute-start.8 = (bf16[16,256,128]{2,1,0:T(8,128)(2,1)S(1)}, bf16[16,256,128]{2,1,0:T(8,128)(2,1)S(1)}, u32[]{:S(2)}, u32[]{:S(2)}) collective-permute-start(bf16[16,256,128]{2,1,0:T(8,128)(2,1)S(1)} %bitcast.24), channel_id=1, source_target_pairs={{0,8},{8,0},{1,9},{9,1},{2,10},{10,2},{3,11},{11,3},{4,12},{12,4},... | collective-permute-start | bytes 3145736 | tf_op jit(solution)/shard_map/ppermute | solution.py:351
  46.6 0.6 stack.58.place_ref
  47.2 0.0 copy-done
  47.2 59.2 %attention.2.refs_0_ = f32[16,4,256]{2,1,0:T(4,128)} custom-call(s32[5]{0:T(128)} %stack.58.place_ref, bf16[16,256,128]{2,1,0:T(8,128)(2,1)} %bitcast.25, bf16[4096,144]{1,0:T(8,128)(2,1)} %key_feats.1.keys), custom_call_target="tpu_custom_call" | custom-call | tf_op jit(solution)/shard_map/attention/pallas_call | solution.py:388
  106.4 0.0 collective-permute-done.8.query_ref
  106.4 0.0 copy-start.1
  106.4 1.0 copy-done.1
  107.4 59.3 %attention.3 = f32[16,2,4,256]{3,2,1,0:T(4,128)} custom-call(s32[5]{0:T(128)} %stack.58.place_ref, bf16[16,256,128]{2,1,0:T(8,128)(2,1)} %copy-done.1, bf16[4096,144]{1,0:T(8,128)(2,1)} %key_feats.1.keys, f32[16,4,256]{2,1,0:T(4,128)} %attention.2.refs_0_), custom_call_target="tpu_custom_call" | custom-call | tf_op jit(solution)/shard_map/attention/pallas_call | solution.py:388
  166.7 7.7 %all-to-all-start = ((f32[32,4,256]{2,1,0:T(4,128)}), f32[32,4,256]{2,1,0:T(4,128)S(1)}, u32[]{:S(2)}, u32[]{:S(2)}) async-start(f32[32,4,256]{2,1,0:T(4,128)} %bitcast.30), calls=%async_computation | async-start | bytes 262144 | tf_op jit(solution)/shard_map/all_to_all | solution.py:409
  174.4 11.3 %all-to-all-done = f32[32,4,256]{2,1,0:T(4,128)S(1)} async-done(((f32[32,4,256]{2,1,0:T(4,128)}), f32[32,4,256]{2,1,0:T(4,128)S(1)}, u32[]{:S(2)}, u32[]{:S(2)}) %all-to-all-start) | async-done | bytes 131104 | tf_op jit(solution)/shard_map/all_to_all | solution.py:409
  185.7 0.1 slice_reduce_fusion
  185.8 0.1 multiply_exponential_fusion
  185.8 0.1 fusion
  185.9 0.6 broadcast_in_dim.5
  186.5 3.5 %all-to-all-start.1 = ((f32[8,4,256]{2,1,0:T(4,128)}), f32[8,4,256]{2,1,0:T(4,128)S(1)}, u32[]{:S(2)}, u32[]{:S(2)}) async-start(f32[8,4,256]{2,1,0:T(4,128)} %broadcast_in_dim.5), calls=%async_computation.1 | async-start | bytes 65536 | tf_op jit(solution)/shard_map/all_to_all | solution.py:411
  190.1 5.1 %all-to-all-done.1 = f32[8,4,256]{2,1,0:T(4,128)S(1)} async-done(((f32[8,4,256]{2,1,0:T(4,128)}), f32[8,4,256]{2,1,0:T(4,128)S(1)}, u32[]{:S(2)}, u32[]{:S(2)}) %all-to-all-start.1) | async-done | bytes 32800 | tf_op jit(solution)/shard_map/all_to_all | solution.py:411
  195.3 0.1 div.38
  195.4 0.1 div.42
  195.5 0.1 broadcast_subtract_fusion
  195.5 0.6 pad_maximum_fusion.3
  (9 shorter events, 0.1 us)
Async XLA Ops:
  3.3 10.2 %collective-permute-start = (bf16[112,512]{1,0:T(8,128)(2,1)}, bf16[112,512]{1,0:T(8,128)(2,1)S(1)}, u32[]{:S(2)}, u32[]{:S(2)}) collective-permute-start(bf16[112,512]{1,0:T(8,128)(2,1)} %get-tuple-element.24), channel_id=1, source_target_pairs={{0,8},{8,16},{16,24},{24,32},{32,40},{40,48},{48,56},{56,64},{64,7... | collective-permute-start | bytes 344072 | tf_op jit(solution)/shard_map/ppermute | solution.py:318
  13.4 0.6 copy-start.2
  15.8 10.7 %collective-permute-start.3 = (bf16[256,128]{1,0:T(8,128)(2,1)}, bf16[256,128]{1,0:T(8,128)(2,1)S(1)}, u32[]{:S(2)}, u32[]{:S(2)}) collective-permute-start(bf16[256,128]{1,0:T(8,128)(2,1)} %get-tuple-element.26), channel_id=1, source_target_pairs={{0,48},{16,0},{32,16},{48,32},{1,49},{17,1},{33,17},{49,33},{2,50}... | collective-permute-start | bytes 196616 | tf_op jit(solution)/shard_map/ppermute | solution.py:338
  18.3 8.2 %collective-permute-start.1 = (bf16[256,128]{1,0:T(8,128)(2,1)}, bf16[256,128]{1,0:T(8,128)(2,1)S(1)}, u32[]{:S(2)}, u32[]{:S(2)}) collective-permute-start(bf16[256,128]{1,0:T(8,128)(2,1)} %get-tuple-element.26), channel_id=1, source_target_pairs={{0,16},{16,32},{32,48},{48,0},{1,17},{17,33},{33,49},{49,1},{2,18}... | collective-permute-start | bytes 196616 | tf_op jit(solution)/shard_map/ppermute | solution.py:338
  20.0 7.4 %collective-permute-start.2 = (bf16[256,128]{1,0:T(8,128)(2,1)}, bf16[256,128]{1,0:T(8,128)(2,1)S(1)}, u32[]{:S(2)}, u32[]{:S(2)}) collective-permute-start(bf16[256,128]{1,0:T(8,128)(2,1)} %get-tuple-element.26), channel_id=1, source_target_pairs={{0,32},{16,48},{32,0},{48,16},{1,33},{17,49},{33,1},{49,17},{2,34}... | collective-permute-start | bytes 196616 | tf_op jit(solution)/shard_map/ppermute | solution.py:338
  23.3 5.0 %collective-permute-start.4 = (bf16[16,768]{1,0:T(8,128)(2,1)}, bf16[16,768]{1,0:T(8,128)(2,1)S(1)}, u32[]{:S(2)}, u32[]{:S(2)}) collective-permute-start(bf16[16,768]{1,0:T(8,128)(2,1)} %get-tuple-element.27), channel_id=1, source_target_pairs={{0,1},{1,2},{2,3},{3,4},{4,5},{5,6},{6,7},{8,9},{9,10},{10,11},{11... | collective-permute-start | bytes 73736 | tf_op jit(solution)/shard_map/ppermute | solution.py:333
  28.3 4.9 %copy-start.3 = (bf16[16,768]{1,0:T(8,128)(2,1)}, bf16[16,768]{1,0:T(8,128)(2,1)S(1)}, u32[]{:S(2)}) copy-start(bf16[16,768]{1,0:T(8,128)(2,1)S(1)} %collective-permute-done.4.side_ref) | copy-start | bytes 73732
  28.3 14.0 %collective-permute-start.5 = (bf16[4,256,128]{2,1,0:T(8,128)(2,1)S(1)}, bf16[4,256,128]{2,1,0:T(8,128)(2,1)S(1)}, u32[]{:S(2)}, u32[]{:S(2)}) collective-permute-start(bf16[4,256,128]{2,1,0:T(8,128)(2,1)S(1)} %pad_maximum_fusion.1), channel_id=1, source_target_pairs={{0,64},{64,128},{128,192},{192,0},{1,65},{65,129},{129,193},{193,1... | collective-permute-start | bytes 786440 | tf_op jit(solution)/shard_map/ppermute | solution.py:338
  29.6 12.7 %collective-permute-start.6 = (bf16[4,256,128]{2,1,0:T(8,128)(2,1)S(1)}, bf16[4,256,128]{2,1,0:T(8,128)(2,1)S(1)}, u32[]{:S(2)}, u32[]{:S(2)}) collective-permute-start(bf16[4,256,128]{2,1,0:T(8,128)(2,1)S(1)} %pad_maximum_fusion.1), channel_id=1, source_target_pairs={{0,128},{64,192},{128,0},{192,64},{1,129},{65,193},{129,1},{193,65... | collective-permute-start | bytes 786440 | tf_op jit(solution)/shard_map/ppermute | solution.py:338
  32.0 10.3 %collective-permute-start.7 = (bf16[4,256,128]{2,1,0:T(8,128)(2,1)S(1)}, bf16[4,256,128]{2,1,0:T(8,128)(2,1)S(1)}, u32[]{:S(2)}, u32[]{:S(2)}) collective-permute-start(bf16[4,256,128]{2,1,0:T(8,128)(2,1)S(1)} %pad_maximum_fusion.1), channel_id=1, source_target_pairs={{0,192},{64,0},{128,64},{192,128},{1,193},{65,1},{129,65},{193,129... | collective-permute-start | bytes 786440 | tf_op jit(solution)/shard_map/ppermute | solution.py:338
  42.4 4.8 %copy-start = (bf16[4,4,256,128]{3,2,1,0:T(8,128)(2,1)}, bf16[4,4,256,128]{3,2,1,0:T(8,128)(2,1)S(1)}, u32[]{:S(2)}) copy-start(bf16[4,4,256,128]{3,2,1,0:T(8,128)(2,1)S(1)} %pad_maximum_fusion) | copy-start | bytes 3145732
  42.4 64.0 %collective-permute-start.8 = (bf16[16,256,128]{2,1,0:T(8,128)(2,1)S(1)}, bf16[16,256,128]{2,1,0:T(8,128)(2,1)S(1)}, u32[]{:S(2)}, u32[]{:S(2)}) collective-permute-start(bf16[16,256,128]{2,1,0:T(8,128)(2,1)S(1)} %bitcast.24), channel_id=1, source_target_pairs={{0,8},{8,0},{1,9},{9,1},{2,10},{10,2},{3,11},{11,3},{4,12},{12,4},... | collective-permute-start | bytes 3145736 | tf_op jit(solution)/shard_map/ppermute | solution.py:351
  106.4 1.0 copy-start.1
  166.7 19.0 %all-to-all-start = ((f32[32,4,256]{2,1,0:T(4,128)}), f32[32,4,256]{2,1,0:T(4,128)S(1)}, u32[]{:S(2)}, u32[]{:S(2)}) async-start(f32[32,4,256]{2,1,0:T(4,128)} %bitcast.30), calls=%async_computation | async-start | bytes 262144 | tf_op jit(solution)/shard_map/all_to_all | solution.py:409
  186.5 8.7 %all-to-all-start.1 = ((f32[8,4,256]{2,1,0:T(4,128)}), f32[8,4,256]{2,1,0:T(4,128)S(1)}, u32[]{:S(2)}, u32[]{:S(2)}) async-start(f32[8,4,256]{2,1,0:T(4,128)} %broadcast_in_dim.5), calls=%async_computation.1 | async-start | bytes 65536 | tf_op jit(solution)/shard_map/all_to_all | solution.py:411

commit v7 on v6

--- a/solution.py
+++ b/solution.py
@@ -241,7 +241,7 @@
                 out_ref[there] = block
 
     sample = jnp.concatenate(
-        [keys[i * tile_cols : i * tile_cols + 16, 0:channels] for i in range(tile_rows)], axis=0
+        [keys[i * tile_cols : i * tile_cols + 16, 0:channels] for i in range(0, tile_rows, 2)], axis=0
     )
     shift = jnp.max(dot(sample, qt[0:channels, :]), axis=0, keepdims=True)
     set_shift(shift)
@@ -316,14 +316,23 @@
         name="query_feats",
     )(frame_band.transpose(1, 0, 2), weights, frame_two, frame_two)
     above = lax.ppermute(down, pb, [(i, i + 1) for i in range(n_pb - 1)])
-    later, edge = lax.optimization_barrier((weights, edge))
+    place = jnp.stack(
+        [
+            pb_index * tile_rows,
+            ka_index * tile_cols,
+            lax.axis_index("core"),
+            lax.axis_index("z"),
+            lax.axis_index("x"),
+        ]
+    ).astype(jnp.int32)
+    later, edge, place = lax.optimization_barrier((weights, edge, place))
     bands = pl.pallas_call(
         weight_kernel,
         out_shape=jax.ShapeDtypeStruct((3, depth, (GROUP // 2 + 1) * channels), BF16),
         compiler_params=params,
         name="key_weights",
     )(later)
-    main, bands = lax.optimization_barrier((main, bands))
+    main, bands, place = lax.optimization_barrier((main, bands, place))
     mine, right = pl.pallas_call(
         join_kernel,
         out_shape=(outs[0], outs[3]),
@@ -350,15 +359,6 @@
     queries, keys = lax.optimization_barrier((queries, keys))
     twins = lax.ppermute(queries, "core", [(0, 1), (1, 0)])
 
-    place = jnp.stack(
-        [
-            pb_index * tile_rows,
-            ka_index * tile_cols,
-            lax.axis_index("core"),
-            lax.axis_index("z"),
-            lax.axis_index("x"),
-        ]
-    ).astype(jnp.int32)
     n_block, n_x = lax.axis_size("z"), lax.axis_size("x")
     scale = math.log2(math.e) / math.sqrt(channels)
 

time: 197 us -> 199 us (1.010)
  waiting for transfers between devices: 17.4 us -> 19.9 us
    ppermute x6, waiting for transfers between devices: 0.91 us -> 3.36 us  [circled(): return jnp.stack([x] + [lax.ppermute(x, axis, pairs) for pairs in turns])]
    ppermute x1, starting transfers between devices: 4.16 us -> 1.83 us  [on_device(): twins = lax.ppermute(queries, 'core', [(0, 1), (1, 0)])]
  transfers between devices with their start and end apart: 11 -> 11, of which waited for: 3 -> 4; matrix products, arithmetic and copies ran while one was open for 1% -> 1% of each run, Pallas kernels for 37% -> 36%
where the time goes in v7:
time: 199 us
  Pallas kernels  136 us (68%)
  starting transfers between devices  37.3 us (19%)
  waiting for transfers between devices  19.9 us (10%)
  local copies, waits for them, and re-layouts  3.07 us (2%)
    pallas_call x2, Pallas kernels, attend(): pl.pallas_call(functools.partial(attention_kernel, tile_rows, float(row_c...  118 us
    ppermute x6, starting transfers between devices, circled(): return jnp.stack([x] + [lax.ppermute(x, axis, pairs) for pairs in turns])  12.4 us
    all_to_all x1, waiting for transfers between devices, on_device(): mine = merged(lax.all_to_all(states, pb, 0, 0), scale)  11.3 us
    pallas_call x1, Pallas kernels, on_device(): pl.pallas_call(key_kernel, out_shape=jax.ShapeDtypeStruct((n_key, channel...  9.05 us
    all_to_all x1, starting transfers between devices, on_device(): mine = merged(lax.all_to_all(states, pb, 0, 0), scale)  8.64 us
    ppermute x1, starting transfers between devices, on_device(): above = lax.ppermute(down, pb, [(i, i + 1) for i in range(n_pb - 1)])  6.29 us
    all_to_all x1, waiting for transfers between devices, on_device(): final = merged(lax.all_to_all(copies, 'ka', 0, 0), scale)  5.15 us
    all_to_all x1, starting transfers between devices, on_device(): final = merged(lax.all_to_all(copies, 'ka', 0, 0), scale)  5.01 us
  transfers between devices with their start and end apart: 11, of which 4 were waited for; matrix products, arithmetic and copies ran while one was open for 1% of the time, Pallas kernels for 36%

profile of v7, /device:TPU:1, one launch (start us, length us, event | category | flops | bytes accessed | tf_op | source)
XLA Modules:
  0.0 198.6 jit_solution(6971388256453202869)
XLA Ops:
  0.0 3.3 %query_feats.1 = (bf16[256,128]{1,0:T(8,128)(2,1)}, f32[8,128]{1,0:T(8,128)}, bf16[112,512]{1,0:T(8,128)(2,1)}, bf16[16,768]{1,0:T(8,128)(2,1)}) custom-call(bf16[9,96,128]{2,1,0:T(8,128)(2,1)} %bitcast.34, bf16[9,96,128]{2,1,0:T(8,128)(2,1)} %bitcast.26, bf16[96,32,512]{2,1,0:T(8,128)(2,1)} %x_ref.1, bf16[96,32,512]{2,1,0:T(8,128)(2,1)} %x_ref.1), custom_call_target="tpu_custom_call" | custom-call | tf_op jit(solution)/shard_map/query_feats/pallas_call | solution.py:304
  3.3 6.3 %collective-permute-start = (bf16[112,512]{1,0:T(8,128)(2,1)}, bf16[112,512]{1,0:T(8,128)(2,1)S(1)}, u32[]{:S(2)}, u32[]{:S(2)}) collective-permute-start(bf16[112,512]{1,0:T(8,128)(2,1)} %get-tuple-element.28), channel_id=1, source_target_pairs={{0,8},{8,16},{16,24},{24,32},{32,40},{40,48},{48,56},{56,64},{64,7... | collective-permute-start | bytes 344072 | tf_op jit(solution)/shard_map/ppermute | solution.py:318
  9.6 0.7 stack.58.place_ref
  10.2 3.9 %key_weights.1.band_ref = bf16[3,768,640]{2,1,0:T(8,128)(2,1)} custom-call(bf16[9,96,128]{2,1,0:T(8,128)(2,1)} %bitcast.27), custom_call_target="tpu_custom_call" | custom-call | tf_op jit(solution)/shard_map/key_weights/pallas_call | solution.py:329
  14.1 0.0 collective-permute-done.down_ref.above_ref
  14.1 0.0 copy-start.2
  14.1 0.6 copy-done.2
  14.8 1.7 query_join.1
  16.5 2.5 %collective-permute-start.3 = (bf16[256,128]{1,0:T(8,128)(2,1)}, bf16[256,128]{1,0:T(8,128)(2,1)S(1)}, u32[]{:S(2)}, u32[]{:S(2)}) collective-permute-start(bf16[256,128]{1,0:T(8,128)(2,1)} %get-tuple-element.30), channel_id=1, source_target_pairs={{0,48},{16,0},{32,16},{48,32},{1,49},{17,1},{33,17},{49,33},{2,50}... | collective-permute-start | bytes 196616 | tf_op jit(solution)/shard_map/ppermute | solution.py:347
  18.9 1.7 collective-permute-start.1
  20.6 3.3 %collective-permute-start.2 = (bf16[256,128]{1,0:T(8,128)(2,1)}, bf16[256,128]{1,0:T(8,128)(2,1)S(1)}, u32[]{:S(2)}, u32[]{:S(2)}) collective-permute-start(bf16[256,128]{1,0:T(8,128)(2,1)} %get-tuple-element.30), channel_id=1, source_target_pairs={{0,32},{16,48},{32,0},{48,16},{1,33},{17,49},{33,1},{49,17},{2,34}... | collective-permute-start | bytes 196616 | tf_op jit(solution)/shard_map/ppermute | solution.py:347
  23.9 3.2 %collective-permute-start.4 = (bf16[16,768]{1,0:T(8,128)(2,1)}, bf16[16,768]{1,0:T(8,128)(2,1)S(1)}, u32[]{:S(2)}, u32[]{:S(2)}) collective-permute-start(bf16[16,768]{1,0:T(8,128)(2,1)} %get-tuple-element.31), channel_id=1, source_target_pairs={{0,1},{1,2},{2,3},{3,4},{4,5},{5,6},{6,7},{8,9},{9,10},{10,11},{11... | collective-permute-start | bytes 73736 | tf_op jit(solution)/shard_map/ppermute | solution.py:342
  27.1 0.0 collective-permute-done.3
  27.2 0.0 collective-permute-done.1
  27.2 2.6 %collective-permute-done.2 = bf16[256,128]{1,0:T(8,128)(2,1)S(1)} collective-permute-done((bf16[256,128]{1,0:T(8,128)(2,1)}, bf16[256,128]{1,0:T(8,128)(2,1)S(1)}, u32[]{:S(2)}, u32[]{:S(2)}) %collective-permute-start.2) | collective-permute-done | bytes 65568 | tf_op jit(solution)/shard_map/ppermute | solution.py:347
  29.8 0.9 pad_maximum_fusion.1
  30.6 0.0 collective-permute-done.4.side_ref
  30.7 0.0 copy-start.3
  30.7 1.3 collective-permute-start.5
  31.9 1.8 collective-permute-start.6
  33.7 1.8 collective-permute-start.7
  35.5 0.0 copy-done.3
  35.5 9.1 %key_feats.1.keys = bf16[4096,144]{1,0:T(8,128)(2,1)} custom-call(bf16[96,32,512]{2,1,0:T(8,128)(2,1)} %x_ref.1, bf16[9,96,128]{2,1,0:T(8,128)(2,1)} %bitcast.28, bf16[3,768,640]{2,1,0:T(8,128)(2,1)} %key_weights.1.band_ref, bf16[112,512]{1,0:T(8,128)(2,1)} %copy-done.2, bf16[16,768]{1,0:T(8,128)(2,1)} %copy-done.3), custom_call_target="tpu_custom_call" | custom-call | tf_op jit(solution)/shard_map/key_feats/pallas_call | solution.py:353
  44.6 0.0 collective-permute-done.5
  44.6 0.0 collective-permute-done.6
  44.6 0.7 collective-permute-done.7
  45.3 0.1 pad_maximum_fusion
  45.5 0.0 copy-start
  45.5 1.8 collective-permute-start.8
  47.3 0.0 copy-done
  47.3 59.1 %attention.2.refs_0_ = f32[16,4,256]{2,1,0:T(4,128)} custom-call(s32[5]{0:T(128)} %stack.58.place_ref, bf16[16,256,128]{2,1,0:T(8,128)(2,1)} %bitcast.25, bf16[4096,144]{1,0:T(8,128)(2,1)} %key_feats.1.keys), custom_call_target="tpu_custom_call" | custom-call | tf_op jit(solution)/shard_map/attention/pallas_call | solution.py:388
  106.5 0.0 collective-permute-done.8.query_ref
  106.5 0.0 copy-start.1
  106.5 1.0 copy-done.1
  107.4 59.2 %attention.3 = f32[16,2,4,256]{3,2,1,0:T(4,128)} custom-call(s32[5]{0:T(128)} %stack.58.place_ref, bf16[16,256,128]{2,1,0:T(8,128)(2,1)} %copy-done.1, bf16[4096,144]{1,0:T(8,128)(2,1)} %key_feats.1.keys, f32[16,4,256]{2,1,0:T(4,128)} %attention.2.refs_0_), custom_call_target="tpu_custom_call" | custom-call | tf_op jit(solution)/shard_map/attention/pallas_call | solution.py:388
  166.7 8.6 %all-to-all-start = ((f32[32,4,256]{2,1,0:T(4,128)}), f32[32,4,256]{2,1,0:T(4,128)S(1)}, u32[]{:S(2)}, u32[]{:S(2)}) async-start(f32[32,4,256]{2,1,0:T(4,128)} %bitcast.30), calls=%async_computation | async-start | bytes 262144 | tf_op jit(solution)/shard_map/all_to_all | solution.py:409
  175.3 11.3 %all-to-all-done = f32[32,4,256]{2,1,0:T(4,128)S(1)} async-done(((f32[32,4,256]{2,1,0:T(4,128)}), f32[32,4,256]{2,1,0:T(4,128)S(1)}, u32[]{:S(2)}, u32[]{:S(2)}) %all-to-all-start) | async-done | bytes 131104 | tf_op jit(solution)/shard_map/all_to_all | solution.py:409
  186.6 0.1 slice_reduce_fusion
  186.7 0.1 multiply_exponential_fusion
  186.8 0.1 fusion
  186.8 0.6 broadcast_in_dim.5
  187.5 5.0 %all-to-all-start.1 = ((f32[8,4,256]{2,1,0:T(4,128)}), f32[8,4,256]{2,1,0:T(4,128)S(1)}, u32[]{:S(2)}, u32[]{:S(2)}) async-start(f32[8,4,256]{2,1,0:T(4,128)} %broadcast_in_dim.5), calls=%async_computation.1 | async-start | bytes 65536 | tf_op jit(solution)/shard_map/all_to_all | solution.py:411
  192.5 5.2 %all-to-all-done.1 = f32[8,4,256]{2,1,0:T(4,128)S(1)} async-done(((f32[8,4,256]{2,1,0:T(4,128)}), f32[8,4,256]{2,1,0:T(4,128)S(1)}, u32[]{:S(2)}, u32[]{:S(2)}) %all-to-all-start.1) | async-done | bytes 32800 | tf_op jit(solution)/shard_map/all_to_all | solution.py:411
  197.7 0.1 div.38
  197.8 0.1 div.42
  197.9 0.1 broadcast_subtract_fusion
  198.0 0.6 pad_maximum_fusion.3
  (9 shorter events, 0.1 us)
Async XLA Ops:
  3.3 10.8 %collective-permute-start = (bf16[112,512]{1,0:T(8,128)(2,1)}, bf16[112,512]{1,0:T(8,128)(2,1)S(1)}, u32[]{:S(2)}, u32[]{:S(2)}) collective-permute-start(bf16[112,512]{1,0:T(8,128)(2,1)} %get-tuple-element.28), channel_id=1, source_target_pairs={{0,8},{8,16},{16,24},{24,32},{32,40},{40,48},{48,56},{56,64},{64,7... | collective-permute-start | bytes 344072 | tf_op jit(solution)/shard_map/ppermute | solution.py:318
  14.1 0.6 copy-start.2
  16.5 10.7 %collective-permute-start.3 = (bf16[256,128]{1,0:T(8,128)(2,1)}, bf16[256,128]{1,0:T(8,128)(2,1)S(1)}, u32[]{:S(2)}, u32[]{:S(2)}) collective-permute-start(bf16[256,128]{1,0:T(8,128)(2,1)} %get-tuple-element.30), channel_id=1, source_target_pairs={{0,48},{16,0},{32,16},{48,32},{1,49},{17,1},{33,17},{49,33},{2,50}... | collective-permute-start | bytes 196616 | tf_op jit(solution)/shard_map/ppermute | solution.py:347
  18.9 8.2 %collective-permute-start.1 = (bf16[256,128]{1,0:T(8,128)(2,1)}, bf16[256,128]{1,0:T(8,128)(2,1)S(1)}, u32[]{:S(2)}, u32[]{:S(2)}) collective-permute-start(bf16[256,128]{1,0:T(8,128)(2,1)} %get-tuple-element.30), channel_id=1, source_target_pairs={{0,16},{16,32},{32,48},{48,0},{1,17},{17,33},{33,49},{49,1},{2,18}... | collective-permute-start | bytes 196616 | tf_op jit(solution)/shard_map/ppermute | solution.py:347
  20.6 9.1 %collective-permute-start.2 = (bf16[256,128]{1,0:T(8,128)(2,1)}, bf16[256,128]{1,0:T(8,128)(2,1)S(1)}, u32[]{:S(2)}, u32[]{:S(2)}) collective-permute-start(bf16[256,128]{1,0:T(8,128)(2,1)} %get-tuple-element.30), channel_id=1, source_target_pairs={{0,32},{16,48},{32,0},{48,16},{1,33},{17,49},{33,1},{49,17},{2,34}... | collective-permute-start | bytes 196616 | tf_op jit(solution)/shard_map/ppermute | solution.py:347
  23.9 6.7 %collective-permute-start.4 = (bf16[16,768]{1,0:T(8,128)(2,1)}, bf16[16,768]{1,0:T(8,128)(2,1)S(1)}, u32[]{:S(2)}, u32[]{:S(2)}) collective-permute-start(bf16[16,768]{1,0:T(8,128)(2,1)} %get-tuple-element.31), channel_id=1, source_target_pairs={{0,1},{1,2},{2,3},{3,4},{4,5},{5,6},{6,7},{8,9},{9,10},{10,11},{11... | collective-permute-start | bytes 73736 | tf_op jit(solution)/shard_map/ppermute | solution.py:342
  30.7 4.9 %copy-start.3 = (bf16[16,768]{1,0:T(8,128)(2,1)}, bf16[16,768]{1,0:T(8,128)(2,1)S(1)}, u32[]{:S(2)}) copy-start(bf16[16,768]{1,0:T(8,128)(2,1)S(1)} %collective-permute-done.4.side_ref) | copy-start | bytes 73732
  30.7 13.9 %collective-permute-start.5 = (bf16[4,256,128]{2,1,0:T(8,128)(2,1)S(1)}, bf16[4,256,128]{2,1,0:T(8,128)(2,1)S(1)}, u32[]{:S(2)}, u32[]{:S(2)}) collective-permute-start(bf16[4,256,128]{2,1,0:T(8,128)(2,1)S(1)} %pad_maximum_fusion.1), channel_id=1, source_target_pairs={{0,64},{64,128},{128,192},{192,0},{1,65},{65,129},{129,193},{193,1... | collective-permute-start | bytes 786440 | tf_op jit(solution)/shard_map/ppermute | solution.py:347
  31.9 12.7 %collective-permute-start.6 = (bf16[4,256,128]{2,1,0:T(8,128)(2,1)S(1)}, bf16[4,256,128]{2,1,0:T(8,128)(2,1)S(1)}, u32[]{:S(2)}, u32[]{:S(2)}) collective-permute-start(bf16[4,256,128]{2,1,0:T(8,128)(2,1)S(1)} %pad_maximum_fusion.1), channel_id=1, source_target_pairs={{0,128},{64,192},{128,0},{192,64},{1,129},{65,193},{129,1},{193,65... | collective-permute-start | bytes 786440 | tf_op jit(solution)/shard_map/ppermute | solution.py:347
  33.7 11.6 %collective-permute-start.7 = (bf16[4,256,128]{2,1,0:T(8,128)(2,1)S(1)}, bf16[4,256,128]{2,1,0:T(8,128)(2,1)S(1)}, u32[]{:S(2)}, u32[]{:S(2)}) collective-permute-start(bf16[4,256,128]{2,1,0:T(8,128)(2,1)S(1)} %pad_maximum_fusion.1), channel_id=1, source_target_pairs={{0,192},{64,0},{128,64},{192,128},{1,193},{65,1},{129,65},{193,129... | collective-permute-start | bytes 786440 | tf_op jit(solution)/shard_map/ppermute | solution.py:347
  45.5 1.8 copy-start
  45.5 61.0 %collective-permute-start.8 = (bf16[16,256,128]{2,1,0:T(8,128)(2,1)S(1)}, bf16[16,256,128]{2,1,0:T(8,128)(2,1)S(1)}, u32[]{:S(2)}, u32[]{:S(2)}) collective-permute-start(bf16[16,256,128]{2,1,0:T(8,128)(2,1)S(1)} %bitcast.24), channel_id=1, source_target_pairs={{0,8},{8,0},{1,9},{9,1},{2,10},{10,2},{3,11},{11,3},{4,12},{12,4},... | collective-permute-start | bytes 3145736 | tf_op jit(solution)/shard_map/ppermute | solution.py:360
  106.5 1.0 copy-start.1
  166.7 20.0 %all-to-all-start = ((f32[32,4,256]{2,1,0:T(4,128)}), f32[32,4,256]{2,1,0:T(4,128)S(1)}, u32[]{:S(2)}, u32[]{:S(2)}) async-start(f32[32,4,256]{2,1,0:T(4,128)} %bitcast.30), calls=%async_computation | async-start | bytes 262144 | tf_op jit(solution)/shard_map/all_to_all | solution.py:409
  187.5 10.2 %all-to-all-start.1 = ((f32[8,4,256]{2,1,0:T(4,128)}), f32[8,4,256]{2,1,0:T(4,128)S(1)}, u32[]{:S(2)}, u32[]{:S(2)}) async-start(f32[8,4,256]{2,1,0:T(4,128)} %broadcast_in_dim.5), calls=%async_computation.1 | async-start | bytes 65536 | tf_op jit(solution)/shard_map/all_to_all | solution.py:411
